TPU v7x, 256 devices: a whole 4x4x8 slice. The times are simulated.
256 devices in a mesh: seq: 32 (over x, z), chan: 8 (over y, core).
Axes of the slice: x: 4, y: 4, z: 8, core: 2. Of those that a mesh axis runs over, the one named last changes fastest.
Arguments:
- projections: bfloat16 [3, 8192, 4096], P(None, 'seq', 'chan'), may hold values from -6 to 6
- short_taps: float32 [3, 7, 4096], P(None, None, 'chan'), may hold values from -2 to 2
- filters: float32 [16, 8192], P('chan', 'seq'), may hold values from -0.0625 to 0.0625
- out_weight: bfloat16 [4096, 4096], P(None, 'chan'), may hold values from -0.09375 to 0.09375
Outputs:
- layer_output: bfloat16 [8192, 4096], P('seq', 'chan')
All inputs are finite; a program needn't handle non-finite values.
Results may differ from a plain program's by a relative error of at most 0.0049.
Values may be sent and summed in bfloat16 or wider, within the bound.
A program may use at most 64 MiB of HBM per device.

v0:
```python
import math

import jax
import jax.numpy as jnp
from jax import lax
from jax.sharding import PartitionSpec as P

TAPS = 7


precise = lax.Precision.HIGHEST


def swapped(value, axis, distance):
    mask = 2**distance
    pairs = [(source, source ^ mask) for source in range(lax.axis_size(axis))]
    return lax.ppermute(value, axis, pairs)


def passed_along(value, axis, steps):
    count = lax.axis_size(axis)
    leading, last = (max(0, -steps), min(count, count - steps))
    return lax.ppermute(value, axis, [(source, source + steps) for source in range(leading, last)])


def rotate(operand, cosine, sine_part):
    real_part = operand[..., 0, :, :]
    imag_part = operand[..., 1, :, :]
    return jnp.stack(
        [real_part * cosine - imag_part * sine_part, real_part * sine_part + imag_part * cosine],
        axis=-3,
    )


def complex_product(left, right):
    left_real = left[..., 0, :, :]
    left_imag = left[..., 1, :, :]
    right_real = right[..., 0, :, :]
    right_imag = right[..., 1, :, :]
    return jnp.stack(
        [
            left_real * right_real - left_imag * right_imag,
            left_real * right_imag + left_imag * right_real,
        ],
        axis=-3,
    )


def short_filter(projections, previous, short_taps):
    row_count = projections.shape[1]
    extended = jnp.concatenate([previous, projections], axis=1).astype(jnp.float32)
    accumulated = jnp.zeros(projections.shape, jnp.float32)
    for tap_index in range(TAPS):
        accumulated = (
            accumulated
            + short_taps[:, tap_index, None, :]
            * extended[:, TAPS - 1 - tap_index : TAPS - 1 - tap_index + row_count, :]
        )
    return accumulated


def split_parity(signal, place, count):
    angles = -math.pi * place.astype(jnp.float32) / count
    shifted = rotate(signal, jnp.cos(angles), jnp.sin(angles))
    return jnp.stack([signal, shifted])


def reverse_bits(place, levels):
    frequency = jnp.zeros((), jnp.int32)
    for bit_number in range(levels):
        frequency = frequency + jnp.left_shift(
            jnp.bitwise_and(jnp.right_shift(place, bit_number), 1), levels - 1 - bit_number
        )
    return frequency


def combine_forward(operand, place, levels):
    for bit_number in range(levels - 1, -1, -1):
        span_size = 1 << bit_number
        partner = swapped(operand, "seq", bit_number)
        upper_half = jnp.bitwise_and(jnp.right_shift(place, bit_number), 1) == 1
        offset = jnp.bitwise_and(place, span_size - 1).astype(jnp.float32)
        angles = -math.pi * offset / span_size
        operand = jnp.where(
            upper_half,
            rotate(partner - operand, jnp.cos(angles), jnp.sin(angles)),
            operand + partner,
        )
    return operand


def combine_inverse(operand, place, levels):
    for bit_number in range(levels):
        span_size = 1 << bit_number
        partner = swapped(operand, "seq", bit_number)
        upper_half = jnp.bitwise_and(jnp.right_shift(place, bit_number), 1) == 1
        offset = jnp.bitwise_and(place, span_size - 1).astype(jnp.float32)
        angles = math.pi * offset / span_size
        cosine = jnp.cos(angles)
        sine_part = jnp.sin(angles)
        operand = jnp.where(
            upper_half,
            partner - rotate(operand, cosine, sine_part),
            operand + rotate(partner, cosine, sine_part),
        )
    return operand


def twiddle(operand, frequency, count, direction):
    row_count = operand.shape[2]
    period = 2 * row_count * count
    orders = 2 * frequency + jnp.arange(2, dtype=jnp.int32)
    positions = jnp.arange(row_count, dtype=jnp.int32)
    phases = orders[:, None] * positions[None, :] % period
    angles = direction * 2.0 * math.pi * phases.astype(jnp.float32) / period
    return rotate(operand, jnp.cos(angles)[:, :, None], jnp.sin(angles)[:, :, None])


def dft_matrix(row_count, direction):
    positions = jnp.arange(row_count, dtype=jnp.int32)
    phases = positions[:, None] * positions[None, :] % row_count
    angles = direction * 2.0 * math.pi * phases.astype(jnp.float32) / row_count
    cosine = jnp.cos(angles)
    sine_part = jnp.sin(angles)
    return jnp.concatenate(
        [
            jnp.concatenate([cosine, -sine_part], axis=1),
            jnp.concatenate([sine_part, cosine], axis=1),
        ],
        axis=0,
    )


def local_transform(operand, matrix):
    row_count = operand.shape[2]
    flattened = operand.reshape(2, 2 * row_count, operand.shape[3])
    result = jnp.einsum("rs,ask->ark", matrix, flattened, precision=precise)
    return result.reshape(operand.shape)


def per_device(projections, short_taps, filters, out_weight):
    row_count = projections.shape[1]
    channels = projections.shape[2]
    groups = filters.shape[0]
    half_group = channels // groups // 2
    count = lax.axis_size("seq")
    place = lax.axis_index("seq")
    levels = count.bit_length() - 1
    previous = passed_along(projections[:, row_count - (TAPS - 1) :, :], "seq", 1)
    filtered = short_filter(projections, previous, short_taps)
    product = filtered[1] * filtered[2]
    signal = (
        product.reshape(row_count, groups, 2, half_group)
        .transpose(2, 0, 1, 3)
        .reshape(2, row_count, groups * half_group)
    )
    kernel = jnp.stack([filters.T, jnp.zeros_like(filters.T)])
    signal_parts = split_parity(signal, place, count)
    kernel_parts = split_parity(kernel, place, count)
    signal_size = signal_parts.shape[2] * signal_parts.shape[3]
    packed = jnp.concatenate(
        [signal_parts.reshape(2, 2, 1, -1), kernel_parts.reshape(2, 2, 1, -1)], axis=3
    )
    packed = combine_forward(packed, place, levels)
    signal_parts = packed[:, :, :, :signal_size].reshape(signal_parts.shape)
    kernel_parts = packed[:, :, :, signal_size:].reshape(kernel_parts.shape)
    frequency = reverse_bits(place, levels)
    forward_matrix = dft_matrix(row_count, -1.0)
    signal_spectrum = local_transform(twiddle(signal_parts, frequency, count, -1.0), forward_matrix)
    kernel_spectrum = local_transform(twiddle(kernel_parts, frequency, count, -1.0), forward_matrix)
    spectrum = complex_product(signal_spectrum, jnp.repeat(kernel_spectrum, half_group, axis=3))
    returned = twiddle(local_transform(spectrum, dft_matrix(row_count, 1.0)), frequency, count, 1.0)
    returned = combine_inverse(returned, place, levels)
    angles = math.pi * place.astype(jnp.float32) / count
    long_part = (returned[0] + rotate(returned[1], jnp.cos(angles), jnp.sin(angles))) / (
        2.0 * row_count * count
    )
    long_part = (
        long_part.reshape(2, row_count, groups, half_group)
        .transpose(1, 2, 0, 3)
        .reshape(row_count, channels)
    )
    gated_rows = (filtered[0] * long_part).astype(jnp.bfloat16)
    layer_output = jnp.dot(
        lax.all_gather(gated_rows, "chan", axis=1, tiled=True),
        out_weight,
        preferred_element_type=jnp.float32,
    )
    return layer_output.astype(jnp.bfloat16)


def solution(mesh):
    return jax.shard_map(
        per_device,
        mesh=mesh,
        in_specs=(P(None, "seq", "chan"), P(None, None, "chan"), P("chan", "seq"), P(None, "chan")),
        out_specs=P("seq", "chan"),
        check_vma=False,
    )
```

profile of v0, /device:TPU:1, one launch (start us, length us, event | category | flops | bytes accessed | tf_op | source)
XLA Modules:
  0.0 464.7 jit_solution(6612058494927921483)
XLA Ops:
  7.5 4.4 collective-permute-start
  16.4 3.3 collective-permute-done
  20.2 4.2 fusion
  26.8 1.6 maximum_maximum_fusion
  28.4 7.8 %collective-permute-start.1 = (f32[2,2,1,66048]{3,1,2,0:T(2,128)S(1)}, f32[2,2,1,66048]{3,1,2,0:T(2,128)S(1)}, u32[]{:S(2)}, u32[]{:S(2)}) collective-permute-start(f32[2,2,1,66048]{3,1,2,0:T(2,128)S(1)} %maximum_maximum_fusion), channel_id=1, source_target_pairs={{0,128},{8,136},{16,144},{24,152},{32,160},{40,168},{48,176},{56,1... | collective-permute-start | bytes 3170312 | tf_op jit(solution)/shard_map/ppermute | solution.py:17
  36.4 22.3 %collective-permute-done.1 = f32[2,2,1,66048]{3,1,2,0:T(2,128)S(1)} collective-permute-done((f32[2,2,1,66048]{3,1,2,0:T(2,128)S(1)}, f32[2,2,1,66048]{3,1,2,0:T(2,128)S(1)}, u32[]{:S(2)}, u32[]{:S(2)}) %collective-permute-start.1) | collective-permute-done | bytes 1056800 | tf_op jit(solution)/shard_map/ppermute | solution.py:17
  58.6 1.8 fusion.41
  61.6 3.3 maximum_select_fusion
  64.9 1.6 collective-permute-start.2
  66.7 22.0 %collective-permute-done.2 = f32[2,2,1,66048]{3,1,2,0:T(2,128)} collective-permute-done((f32[2,2,1,66048]{3,1,2,0:T(2,128)}, f32[2,2,1,66048]{3,1,2,0:T(2,128)}, u32[]{:S(2)}, u32[]{:S(2)}) %collective-permute-start.2) | collective-permute-done | bytes 1056800 | tf_op jit(solution)/shard_map/ppermute | solution.py:17
  88.7 3.8 fusion.42
  93.6 2.9 maximum_select_fusion.1
  96.5 2.8 collective-permute-start.3
  99.5 48.5 %collective-permute-done.3 = f32[2,2,1,66048]{3,1,2,0:T(2,128)S(1)} collective-permute-done((f32[2,2,1,66048]{3,1,2,0:T(2,128)S(1)}, f32[2,2,1,66048]{3,1,2,0:T(2,128)S(1)}, u32[]{:S(2)}, u32[]{:S(2)}) %collective-permute-start.3) | collective-permute-done | bytes 1056800 | tf_op jit(solution)/shard_map/ppermute | solution.py:17
  151.4 44.2 %collective-permute-done.4 = f32[2,2,1,66048]{3,1,2,0:T(2,128)S(1)} collective-permute-done((f32[2,2,1,66048]{3,1,2,0:T(2,128)S(1)}, f32[2,2,1,66048]{3,1,2,0:T(2,128)S(1)}, u32[]{:S(2)}, u32[]{:S(2)}) %collective-permute-start.4) | collective-permute-done | bytes 1056800 | tf_op jit(solution)/shard_map/ppermute | solution.py:17
  199.0 1.7 fusion.26
  201.6 1.8 multiply_sine_fusion.1
  203.4 1.8 multiply_sine_fusion
  205.3 18.0 %collective-permute-done.5 = f32[2,2,1,66048]{3,1,2,0:T(2,128)S(1)} collective-permute-done((f32[2,2,1,66048]{3,1,2,0:T(2,128)S(1)}, f32[2,2,1,66048]{3,1,2,0:T(2,128)S(1)}, u32[]{:S(2)}, u32[]{:S(2)}) %collective-permute-start.5) | collective-permute-done | bytes 1056800 | tf_op jit(solution)/shard_map/ppermute | solution.py:17
  231.1 3.6 convolution_bitcast_fusion.1
  239.3 1.9 convolution_bitcast_fusion
  242.3 22.9 %collective-permute-done.6 = f32[2,2,256,256]{3,2,1,0:T(8,128)S(1)} collective-permute-done((f32[2,2,256,256]{3,2,1,0:T(8,128)S(1)}, f32[2,2,256,256]{3,2,1,0:T(8,128)S(1)}, u32[]{:S(2)}, u32[]{:S(2)}) %collective-permute-start.6) | collective-permute-done | bytes 1048608 | tf_op jit(solution)/shard_map/ppermute | solution.py:17
  268.3 46.7 %collective-permute-done.7 = f32[2,2,256,256]{3,2,1,0:T(8,128)S(1)} collective-permute-done((f32[2,2,256,256]{3,2,1,0:T(8,128)}, f32[2,2,256,256]{3,2,1,0:T(8,128)S(1)}, u32[]{:S(2)}, u32[]{:S(2)}) %collective-permute-start.7) | collective-permute-done | bytes 1048608 | tf_op jit(solution)/shard_map/ppermute | solution.py:17
  316.0 1.7 fusion.13
  317.7 2.6 collective-permute-start.8
  320.6 48.2 %collective-permute-done.8 = f32[2,2,256,256]{3,2,1,0:T(8,128)S(1)} collective-permute-done((f32[2,2,256,256]{3,2,1,0:T(8,128)S(1)}, f32[2,2,256,256]{3,2,1,0:T(8,128)S(1)}, u32[]{:S(2)}, u32[]{:S(2)}) %collective-permute-start.8) | collective-permute-done | bytes 1048608 | tf_op jit(solution)/shard_map/ppermute | solution.py:17
  370.8 22.7 %collective-permute-done.9 = f32[2,2,256,256]{3,2,1,0:T(8,128)S(1)} collective-permute-done((f32[2,2,256,256]{3,2,1,0:T(8,128)S(1)}, f32[2,2,256,256]{3,2,1,0:T(8,128)S(1)}, u32[]{:S(2)}, u32[]{:S(2)}) %collective-permute-start.9) | collective-permute-done | bytes 1048608 | tf_op jit(solution)/shard_map/ppermute | solution.py:17
  393.9 3.1 collective-permute-start.10
  397.5 21.6 %collective-permute-done.10 = f32[2,2,256,256]{3,2,1,0:T(8,128)S(1)} collective-permute-done((f32[2,2,256,256]{3,2,1,0:T(8,128)S(1)}, f32[2,2,256,256]{3,2,1,0:T(8,128)S(1)}, u32[]{:S(2)}, u32[]{:S(2)}) %collective-permute-start.10) | collective-permute-done | bytes 1048608 | tf_op jit(solution)/shard_map/ppermute | solution.py:17
  422.1 1.8 fusion.18
  424.0 28.9 %all-gather.2.cloned.1.call-done = bf16[256,4096]{0,1:T(8,128)(2,1)} async-done(((bf16[256,512]{0,1:T(8,128)(2,1)}), bf16[256,4096]{0,1:T(8,128)(2,1)}) %all-gather.2.cloned.1.call-update) | async-done | bytes 2097168 | tf_op jit(solution)/shard_map/all_gather | solution.py:185
  452.8 4.8 %convolution_convert_fusion = bf16[256,512]{1,0:T(8,128)(2,1)} fusion(bf16[256,4096]{0,1:T(8,128)(2,1)} %all-gather.2.cloned.1.call-done, bf16[4096,512]{1,0:T(8,128)(2,1)} %param.7), kind=kOutput, calls=%fused_computation.15 | convolution fusion | flops 1073872896 | bytes 6553600 | tf_op jit(solution)/shard_map/dot_general | solution.py:184
  (127 shorter events, 40.5 us)
Async XLA Ops:
  6.5 446.3 %all-gather.2.cloned.1.call-start = ((), (), s32[]{:S(2)}) async-start(), calls=%async_computation | async-start | bytes 2359296 | tf_op jit(solution)/shard_map/all_gather | solution.py:185
  7.5 12.1 %collective-permute-start = (bf16[3,6,512]{1,2,0:T(8,128)(2,1)S(1)}, bf16[3,6,512]{1,2,0:T(8,128)(2,1)S(1)}, u32[]{:S(2)}, u32[]{:S(2)}) collective-permute-start(bf16[3,6,512]{1,2,0:T(8,128)(2,1)S(1)} %copy.48), channel_id=1, source_target_pairs={{0,8},{8,16},{16,24},{24,32},{32,40},{40,48},{48,56},{56,64},{64,7... | collective-permute-start | bytes 55304 | tf_op jit(solution)/shard_map/ppermute | solution.py:23
  14.1 2.0 copy-start.17
  24.4 1.2 copy-start
  28.4 30.2 %collective-permute-start.1 = (f32[2,2,1,66048]{3,1,2,0:T(2,128)S(1)}, f32[2,2,1,66048]{3,1,2,0:T(2,128)S(1)}, u32[]{:S(2)}, u32[]{:S(2)}) collective-permute-start(f32[2,2,1,66048]{3,1,2,0:T(2,128)S(1)} %maximum_maximum_fusion), channel_id=1, source_target_pairs={{0,128},{8,136},{16,144},{24,152},{32,160},{40,168},{48,176},{56,1... | collective-permute-start | bytes 3170312 | tf_op jit(solution)/shard_map/ppermute | solution.py:17
  64.9 23.8 %collective-permute-start.2 = (f32[2,2,1,66048]{3,1,2,0:T(2,128)}, f32[2,2,1,66048]{3,1,2,0:T(2,128)}, u32[]{:S(2)}, u32[]{:S(2)}) collective-permute-start(f32[2,2,1,66048]{3,1,2,0:T(2,128)} %maximum_select_fusion), channel_id=1, source_target_pairs={{0,64},{8,72},{16,80},{24,88},{32,96},{40,104},{48,112},{56,120},{... | collective-permute-start | bytes 3170312 | tf_op jit(solution)/shard_map/ppermute | solution.py:17
  96.5 51.5 %collective-permute-start.3 = (f32[2,2,1,66048]{3,1,2,0:T(2,128)S(1)}, f32[2,2,1,66048]{3,1,2,0:T(2,128)S(1)}, u32[]{:S(2)}, u32[]{:S(2)}) collective-permute-start(f32[2,2,1,66048]{3,1,2,0:T(2,128)S(1)} %maximum_select_fusion.1), channel_id=1, source_target_pairs={{0,32},{8,40},{16,48},{24,56},{32,0},{40,8},{48,16},{56,24},{64,96... | collective-permute-start | bytes 3170312 | tf_op jit(solution)/shard_map/ppermute | solution.py:17
  151.1 44.5 %collective-permute-start.4 = (f32[2,2,1,66048]{3,1,2,0:T(2,128)S(1)}, f32[2,2,1,66048]{3,1,2,0:T(2,128)S(1)}, u32[]{:S(2)}, u32[]{:S(2)}) collective-permute-start(f32[2,2,1,66048]{3,1,2,0:T(2,128)S(1)} %maximum_select_fusion.2), channel_id=1, source_target_pairs={{0,16},{8,24},{16,0},{24,8},{32,48},{40,56},{48,32},{56,40},{64,80... | collective-permute-start | bytes 3170312 | tf_op jit(solution)/shard_map/ppermute | solution.py:17
  198.6 24.7 %collective-permute-start.5 = (f32[2,2,1,66048]{3,1,2,0:T(2,128)S(1)}, f32[2,2,1,66048]{3,1,2,0:T(2,128)S(1)}, u32[]{:S(2)}, u32[]{:S(2)}) collective-permute-start(f32[2,2,1,66048]{3,1,2,0:T(2,128)S(1)} %maximum_select_fusion.3), channel_id=1, source_target_pairs={{0,8},{8,0},{16,24},{24,16},{32,40},{40,32},{48,56},{56,48},{64,72... | collective-permute-start | bytes 3170312 | tf_op jit(solution)/shard_map/ppermute | solution.py:17
  226.3 1.0 copy-start.9
  227.7 1.0 copy-start.14
  227.8 1.0 copy-start.15
  227.8 1.1 copy-start.16
  228.3 1.5 slice-start
  238.3 1.0 copy-start.12
  238.3 1.0 copy-start.13
  241.7 23.6 %copy-start.1 = (f32[2,1,256,256]{3,2,1,0:T(8,128)}, f32[2,1,256,256]{3,2,1,0:T(8,128)S(1)}, u32[]{:S(2)}) copy-start(f32[2,1,256,256]{3,2,1,0:T(8,128)S(1)} %get-tuple-element.5) | copy-start | bytes 1572868
  241.8 23.4 %collective-permute-start.6 = (f32[2,2,256,256]{3,2,1,0:T(8,128)S(1)}, f32[2,2,256,256]{3,2,1,0:T(8,128)S(1)}, u32[]{:S(2)}, u32[]{:S(2)}) collective-permute-start(f32[2,2,256,256]{3,2,1,0:T(8,128)S(1)} %pad_maximum_fusion.2), channel_id=1, source_target_pairs={{0,8},{8,0},{16,24},{24,16},{32,40},{40,32},{48,56},{56,48},{64,72... | collective-permute-start | bytes 3145736 | tf_op jit(solution)/shard_map/ppermute | solution.py:17
  242.3 24.4 %copy-start.3 = (f32[2,1,256,256]{3,2,1,0:T(8,128)}, f32[2,1,256,256]{3,2,1,0:T(8,128)S(1)}, u32[]{:S(2)}) copy-start(f32[2,1,256,256]{3,2,1,0:T(8,128)S(1)} %multiply_add_fusion.14) | copy-start | bytes 1572868
  265.3 1.4 copy-start.5
  265.3 1.4 copy-start.7
  266.7 48.3 %collective-permute-start.7 = (f32[2,2,256,256]{3,2,1,0:T(8,128)}, f32[2,2,256,256]{3,2,1,0:T(8,128)S(1)}, u32[]{:S(2)}, u32[]{:S(2)}) collective-permute-start(f32[2,2,256,256]{3,2,1,0:T(8,128)} %fusion.12), channel_id=1, source_target_pairs={{0,16},{8,24},{16,0},{24,8},{32,48},{40,56},{48,32},{56,40},{64,80... | collective-permute-start | bytes 3145736 | tf_op jit(solution)/shard_map/ppermute | solution.py:17
  268.3 47.7 %copy-start.2 = (f32[2,1,256,256]{3,2,1,0:T(8,128)S(1)}, f32[2,1,256,256]{3,2,1,0:T(8,128)}, u32[]{:S(2)}) copy-start(f32[2,1,256,256]{3,2,1,0:T(8,128)} %copy-done.1) | copy-start | bytes 1572868
  268.3 47.7 %copy-start.4 = (f32[2,1,256,256]{3,2,1,0:T(8,128)S(1)}, f32[2,1,256,256]{3,2,1,0:T(8,128)}, u32[]{:S(2)}) copy-start(f32[2,1,256,256]{3,2,1,0:T(8,128)} %copy-done.3) | copy-start | bytes 1572868
  268.3 47.7 %copy-start.6 = (f32[2,1,256,256]{3,2,1,0:T(8,128)S(1)}, f32[2,1,256,256]{3,2,1,0:T(8,128)}, u32[]{:S(2)}) copy-start(f32[2,1,256,256]{3,2,1,0:T(8,128)} %copy-done.5) | copy-start | bytes 1572868
  268.3 47.7 %copy-start.8 = (f32[2,1,256,256]{3,2,1,0:T(8,128)S(1)}, f32[2,1,256,256]{3,2,1,0:T(8,128)}, u32[]{:S(2)}) copy-start(f32[2,1,256,256]{3,2,1,0:T(8,128)} %copy-done.7) | copy-start | bytes 1572868
  315.0 1.0 copy-start.10
  317.7 51.0 %collective-permute-start.8 = (f32[2,2,256,256]{3,2,1,0:T(8,128)S(1)}, f32[2,2,256,256]{3,2,1,0:T(8,128)S(1)}, u32[]{:S(2)}, u32[]{:S(2)}) collective-permute-start(f32[2,2,256,256]{3,2,1,0:T(8,128)S(1)} %fusion.13), channel_id=1, source_target_pairs={{0,32},{8,40},{16,48},{24,56},{32,0},{40,8},{48,16},{56,24},{64,96... | collective-permute-start | bytes 3145736 | tf_op jit(solution)/shard_map/ppermute | solution.py:17
  369.2 24.3 %collective-permute-start.9 = (f32[2,2,256,256]{3,2,1,0:T(8,128)S(1)}, f32[2,2,256,256]{3,2,1,0:T(8,128)S(1)}, u32[]{:S(2)}, u32[]{:S(2)}) collective-permute-start(f32[2,2,256,256]{3,2,1,0:T(8,128)S(1)} %fusion.14), channel_id=1, source_target_pairs={{0,64},{8,72},{16,80},{24,88},{32,96},{40,104},{48,112},{56,120},{... | collective-permute-start | bytes 3145736 | tf_op jit(solution)/shard_map/ppermute | solution.py:17
  393.9 25.2 %collective-permute-start.10 = (f32[2,2,256,256]{3,2,1,0:T(8,128)S(1)}, f32[2,2,256,256]{3,2,1,0:T(8,128)S(1)}, u32[]{:S(2)}, u32[]{:S(2)}) collective-permute-start(f32[2,2,256,256]{3,2,1,0:T(8,128)S(1)} %fusion.15), channel_id=1, source_target_pairs={{0,128},{8,136},{16,144},{24,152},{32,160},{40,168},{48,176},{56,1... | collective-permute-start | bytes 3145736 | tf_op jit(solution)/shard_map/ppermute | solution.py:17
  419.5 1.0 copy-start.11
  420.5 1.0 slice-start.1
Sparse Core Ops, SparseCore 0:
  424.1 28.6 all-gather.1
where the time goes:
time: 472 us; the launch traced here: 465 us
  waiting for transfers between devices  349 us (74%)
  other arithmetic  48.4 us (10%)
  starting transfers between devices  24.4 us (5%)
  between operations  16 us (3%)
  local copies, waits for them, and re-layouts  15.4 us (3%)
  matrix products  11.2 us (2%)
    ppermute x10, waiting for transfers between devices, swapped(): return lax.ppermute(value, axis, pairs)  317 us
    all_gather x1, waiting for transfers between devices, per_device(): lax.all_gather(gated_rows, 'chan', axis=1, tiled=True)  28.9 us
    ppermute x10, starting transfers between devices, swapped(): return lax.ppermute(value, axis, pairs)  20 us
    select_n x5, other arithmetic, combine_forward(): jnp.where(upper_half, rotate(partner - operand, jnp.cos(angles), jnp.sin(...  10.6 us
  transfers between devices with their start and end apart: 12, of which 12 were waited for; matrix products, arithmetic and copies ran while one was open for 3% of the time, Pallas kernels for 0%

commit v1 on v0

v1 whole, which is shorter than its diff:
```python
import functools

import jax
import jax.numpy as jnp
from jax import lax
from jax.experimental import pallas as pl
from jax.experimental.pallas import tpu as pltpu
from jax.sharding import PartitionSpec as P

MESH = pl.DeviceIdType.MESH
TAPS = 7
PAD = 16
LANES = 128


def kernel(
    sizes,
    proj_hbm,
    taps_ref,
    filt_ref,
    weight_hbm,
    out_ref,
    proj,
    halo,
    ext,
    filt_all,
    high,
    low,
    product_out,
    product_in,
    total,
    conv_out,
    conv_in,
    query,
    gated,
    weight,
    out_total,
    load_sem,
    self_sem,
    halo_sem,
    filt_sem,
    product_sem,
    conv_send,
    conv_recv,
    gated_send,
    gated_recv,
):
    count, planes, rings = sizes
    rows = proj.shape[1]
    channels = proj.shape[2]
    share = channels // count
    blocks = channels // LANES
    per_block = count // blocks
    me = lax.axis_index("seq")
    chan = lax.axis_index("chan")
    x, z = me // rings, lax.rem(me, rings)
    y, core = chan // 2, lax.rem(chan, 2)
    heights = lax.axis_size("chan") // 2
    step_up = 1 - 2 * core
    down = lax.rem(y + step_up + heights, heights) * 2 + core
    up = lax.rem(y - step_up + heights, heights) * 2 + core
    far = lax.rem(y + 2, heights) * 2 + core
    sibling = y * 2 + 1 - core
    following = lax.rem(me + 1, count)
    group_of = me // (count // filt_ref.shape[0])

    load = pltpu.make_async_copy(proj_hbm, proj, load_sem.at[0])
    load.start()
    load_weight = pltpu.make_async_copy(weight_hbm, weight, load_sem.at[1])
    load_weight.start()

    barrier = pltpu.get_barrier_semaphore()

    def peer(k):
        px = lax.rem(x + k // rings, planes)
        pz = lax.rem(z + lax.rem(k, rings), rings)
        return px * rings + pz

    def greet(k, carry):
        pl.semaphore_signal(barrier, inc=1, device_id={"seq": peer(k)}, device_id_type=MESH)
        return carry

    lax.fori_loop(1, count, greet, 0)
    for other in (down, up, sibling):
        pl.semaphore_signal(barrier, inc=1, device_id={"chan": other}, device_id_type=MESH)
    pl.semaphore_wait(barrier, count + 2)

    halo_copy = pltpu.make_async_remote_copy(
        src_ref=proj_hbm.at[:, pl.ds(rows - PAD, PAD), :],
        dst_ref=halo,
        send_sem=halo_sem.at[0],
        recv_sem=halo_sem.at[1],
        device_id={"seq": following},
        device_id_type=MESH,
    )
    halo_copy.start()

    def send_filter(k, carry):
        pltpu.make_async_remote_copy(
            src_ref=filt_ref,
            dst_ref=filt_all.at[me + 1],
            send_sem=filt_sem.at[0],
            recv_sem=filt_sem.at[1],
            device_id={"seq": peer(k)},
            device_id_type=MESH,
        ).start()
        return carry

    lax.fori_loop(1, count, send_filter, 0)
    pltpu.make_async_copy(filt_ref, filt_all.at[me + 1], filt_sem.at[1]).start()
    filt_all[0] = jnp.zeros(filt_all.shape[1:], jnp.float32)

    load.wait()

    def widen(i, carry):
        s, q = i // blocks, lax.rem(i, blocks)
        lanes = pl.ds(pl.multiple_of(q * LANES, LANES), LANES)
        ext[s, q, pl.ds(PAD, rows), :] = proj[s, :, lanes].astype(jnp.float32)
        return carry

    lax.fori_loop(0, 3 * blocks, widen, 0)

    def short(s, q, first):
        lanes = pl.ds(pl.multiple_of(q * LANES, LANES), LANES)
        taps = taps_ref[s, :, lanes]
        value = taps[0:1, :] * ext[s, q, pl.ds(first + PAD, LANES), :]
        for j in range(1, TAPS):
            value = value + taps[j : j + 1, :] * ext[s, q, pl.ds(first + PAD - j, LANES), :]
        return value

    def products(first):
        def one(q, carry):
            value = short(1, q, first) * short(2, q, first)
            out_rows = pl.ds(pl.multiple_of(q * LANES, LANES), LANES)
            product_out[out_rows, first : first + LANES] = value.T.astype(jnp.bfloat16)
            return carry

        lax.fori_loop(0, blocks, one, 0)

        def send(k, carry):
            to = peer(k)
            pltpu.make_async_remote_copy(
                src_ref=product_out.at[pl.ds(to * share, share), pl.ds(first, LANES)],
                dst_ref=product_in.at[pl.ds(me * share, share), pl.ds(first, LANES)],
                send_sem=product_sem.at[0],
                recv_sem=product_sem.at[1],
                device_id={"seq": to},
                device_id_type=MESH,
            ).start()
            return carry

        lax.fori_loop(1, count, send, 0)
        mine = pl.ds(me * share, share)
        pltpu.make_async_copy(
            product_out.at[mine, pl.ds(first, LANES)],
            product_in.at[mine, pl.ds(first, LANES)],
            product_sem.at[1],
        ).start()

    products(LANES)
    halo_copy.wait()

    def extend(i, carry):
        s, q = i // blocks, lax.rem(i, blocks)
        lanes = pl.ds(pl.multiple_of(q * LANES, LANES), LANES)
        before = halo[s, :, lanes].astype(jnp.float32)
        ext[s, q, 0:PAD, :] = jnp.where(me == 0, 0.0, before)
        return carry

    lax.fori_loop(0, 3 * blocks, extend, 0)
    products(0)

    def queries(q, carry):
        for first in (0, LANES):
            query[q, first : first + LANES, :] = short(0, q, first)
        return carry

    lax.fori_loop(0, blocks, queries, 0)

    pltpu.make_async_copy(filt_all.at[pl.ds(1, count)], filt_all.at[pl.ds(1, count)], filt_sem.at[1]).wait()
    corner = jnp.zeros((LANES, LANES), jnp.bfloat16)
    high[0, LANES:, 0:LANES] = corner
    low[0, LANES:, 0:LANES] = corner

    def spread(d, carry):
        before, here = filt_all[d], filt_all[d + 1]
        line = jnp.concatenate([before[:, rows - LANES :], here], axis=1)
        line = jnp.where(group_of == 0, line[0:1], line[1:2])
        wide = jnp.broadcast_to(line, (LANES, line.shape[1]))
        value = pltpu.roll(wide, 0, 1, stride=1, stride_axis=0)[:, LANES:]
        top = value.astype(jnp.bfloat16)
        rest = (value - top.astype(jnp.float32)).astype(jnp.bfloat16)
        for table, part in ((high, top), (low, rest)):
            table[d, 0:LANES, :] = part
            table[d, LANES:, LANES:] = part[:, :LANES]
            table[d + 1, LANES:, :LANES] = part[:, LANES:]
        return carry

    lax.fori_loop(0, count, spread, 0)

    pltpu.make_async_copy(product_in, product_in, product_sem.at[1]).wait()
    for d in range(count):
        left = product_in[0 : channels - share * d, :]
        part = jnp.dot(left, high[d], preferred_element_type=jnp.float32)
        part = part + jnp.dot(left, low[d], preferred_element_type=jnp.float32)
        if d == 0:
            total[...] = part
        else:
            total[share * d :, :] += part
    conv_out[...] = total[...].astype(jnp.bfloat16)

    def send_back(k, carry):
        to = peer(k)
        pltpu.make_async_remote_copy(
            src_ref=conv_out.at[pl.ds(to * share, share), :],
            dst_ref=conv_in.at[pl.ds(me * share, share), :],
            send_sem=conv_send.at[0],
            recv_sem=conv_recv.at[me // per_block],
            device_id={"seq": to},
            device_id_type=MESH,
        ).start()
        return carry

    mine = pl.ds(me * share, share)
    pltpu.make_async_copy(conv_out.at[mine], conv_in.at[mine], conv_recv.at[me // per_block]).start()
    lax.fori_loop(1, count, send_back, 0)

    def pass_on(source, block, to):
        pltpu.make_async_remote_copy(
            src_ref=gated.at[source, block],
            dst_ref=gated.at[source, block],
            send_sem=gated_send.at[0],
            recv_sem=gated_recv.at[source, block],
            device_id={"chan": to},
            device_id_type=MESH,
        ).start()

    def arrived(source, block):
        slot = gated.at[source, block]
        pltpu.make_async_copy(slot, slot, gated_recv.at[source, block]).wait()

    def block_at(k):
        return lax.rem(x + blocks - k, blocks)

    def gate(k):
        block = block_at(k)
        part = pl.ds(pl.multiple_of(block * LANES, LANES), LANES)
        pltpu.make_async_copy(conv_in.at[part], conv_in.at[part], conv_recv.at[block]).wait()
        value = conv_in[part, :].astype(jnp.float32).T
        gated[chan, block] = (value * query[block]).astype(jnp.bfloat16)
        for to in (down, up, sibling):
            pass_on(chan, block, to)

    def relay_near(k):
        block = block_at(k)
        arrived(up, block)
        pass_on(up, block, down)
        pass_on(up, block, sibling)
        arrived(down, block)
        pass_on(down, block, sibling)

    def relay_far(k):
        block = block_at(k)
        arrived(far, block)
        pass_on(far, block, sibling)

    def project(k):
        block = block_at(k)
        for offset in range(heights):
            arrived(lax.rem(y + offset, heights) * 2 + 1 - core, block)
        left = jnp.concatenate([gated[c, block] for c in range(2 * heights)], axis=1)
        right = jnp.concatenate(
            [
                weight[pl.ds(pl.multiple_of(c * channels + block * LANES, LANES), LANES), :]
                for c in range(2 * heights)
            ],
            axis=0,
        )
        part = jnp.dot(left, right, preferred_element_type=jnp.float32)
        if k == 0:
            out_total[...] = part
        elif k < blocks - 1:
            out_total[...] += part
        else:
            out_ref[...] = (out_total[...] + part).astype(jnp.bfloat16)

    for k in range(blocks + 3):
        if k < blocks:
            gate(k)
        if 1 <= k <= blocks:
            relay_near(k - 1)
        if 2 <= k <= blocks + 1:
            relay_far(k - 2)
        if k == 3:
            load_weight.wait()
        if k >= 3:
            project(k - 3)

    halo_rest = product_out.at[pl.ds(0, (count - 1) * share), :]
    pltpu.make_async_copy(halo_rest, halo_rest, product_sem.at[0]).wait()
    pltpu.make_async_copy(halo_rest, halo_rest, conv_send.at[0]).wait()
    filters_sent = filt_all.at[pl.ds(1, count - 1)]
    pltpu.make_async_copy(filters_sent, filters_sent, filt_sem.at[0]).wait()
    gated_sent = gated.at[pl.ds(0, 7)]
    pltpu.make_async_copy(gated_sent, gated_sent, gated_send.at[0]).wait()


def solution(mesh):
    count = mesh.shape["seq"]
    chans = mesh.shape["chan"]
    planes, rings = 4, count // 4

    def per_device(projections, short_taps, filters, out_weight):
        rows, channels = projections.shape[1], projections.shape[2]
        blocks = channels // LANES
        vmem = pl.BlockSpec(memory_space=pltpu.VMEM)
        hbm = pl.BlockSpec(memory_space=pl.ANY)
        bf16, f32 = jnp.bfloat16, jnp.float32
        dma = pltpu.SemaphoreType.DMA
        return pl.pallas_call(
            functools.partial(kernel, (count, planes, rings)),
            out_shape=jax.ShapeDtypeStruct((rows, out_weight.shape[1]), bf16),
            in_specs=[hbm, vmem, vmem, hbm],
            out_specs=vmem,
            scratch_shapes=[
                pltpu.VMEM(projections.shape, bf16),
                pltpu.VMEM((3, PAD, channels), bf16),
                pltpu.VMEM((3, blocks, PAD + rows, LANES), f32),
                pltpu.VMEM((count + 1, filters.shape[0], rows), f32),
                pltpu.VMEM((count + 1, rows, rows), bf16),
                pltpu.VMEM((count + 1, rows, rows), bf16),
                pltpu.VMEM((channels, rows), bf16),
                pltpu.VMEM((channels, rows), bf16),
                pltpu.VMEM((channels, rows), f32),
                pltpu.VMEM((channels, rows), bf16),
                pltpu.VMEM((channels, rows), bf16),
                pltpu.VMEM((blocks, rows, LANES), f32),
                pltpu.VMEM((chans, blocks, rows, LANES), bf16),
                pltpu.VMEM(out_weight.shape, bf16),
                pltpu.VMEM((rows, out_weight.shape[1]), f32),
                dma((2,)),
                dma((1,)),
                dma((2,)),
                dma((2,)),
                dma((2,)),
                dma((1,)),
                dma((blocks,)),
                dma((1,)),
                dma((chans, blocks)),
            ],
            compiler_params=pltpu.CompilerParams(
                collective_id=0, has_side_effects=True, vmem_limit_bytes=56 * 2**20
            ),
        )(projections, short_taps, filters, out_weight)

    return jax.shard_map(
        per_device,
        mesh=mesh,
        in_specs=(P(None, "seq", "chan"), P(None, None, "chan"), P("chan", "seq"), P(None, "chan")),
        out_specs=P("seq", "chan"),
        check_vma=False,
    )
```

time: 472 us -> 53.4 us (0.11); the launches traced: 465 us -> 53.2 us
  waiting for transfers between devices: 349 us -> 0 us
  Pallas kernels: 0 us -> 51.5 us
  other arithmetic: 48.4 us -> 0 us
  starting transfers between devices: 24.4 us -> 0 us
  between operations: 16 us -> 0.01 us
  local copies, waits for them, and re-layouts: 15.4 us -> 1.67 us
  matrix products: 11.2 us -> 0 us
    ppermute x11 -> x0, waiting for transfers between devices: 320 us -> none  [the longest x10 317 us: swapped(): return lax.ppermute(value, axis, pairs)]
    pallas_call x0 -> x1, Pallas kernels: none -> 51.5 us  [per_device(): pl.pallas_call(functools.partial(kernel, (count, planes, rings)), out_sha...]
    all_gather x1 -> x0, waiting for transfers between devices: 28.9 us -> none  [per_device(): lax.all_gather(gated_rows, 'chan', axis=1, tiled=True)]
    ppermute x11 -> x0, starting transfers between devices: 24.4 us -> none  [the longest x10 20 us: swapped(): return lax.ppermute(value, axis, pairs)]
    sub x26 -> x0, other arithmetic: 17.8 us -> none  [the longest x20 8.91 us: rotate(): real_part * cosine - imag_part * sine_part]
    select_n x10 -> x0, other arithmetic: 14.6 us -> none  [the longest x5 10.6 us: combine_forward(): jnp.where(upper_half, rotate(partner - operand, jnp.cos(angles), jnp.sin(...]
    dot_general x4 -> x0, matrix products: 11.2 us -> none  [the longest x3 6.41 us: local_transform(): result = jnp.einsum('rs,ask->ark', matrix, flattened, precision=precise)]
  transfers between devices with their start and end apart: 12 -> 0, of which waited for: 12 -> 0; matrix products, arithmetic and copies ran while one was open for 3% -> 0% of each run, Pallas kernels for 0% -> 0%
where the time goes in v1:
time: 53.4 us; the launch traced here: 53.2 us
  Pallas kernels  51.5 us (96%)
  local copies, waits for them, and re-layouts  1.67 us (3%)
    pallas_call x1, Pallas kernels, per_device(): pl.pallas_call(functools.partial(kernel, (count, planes, rings)), out_sha...  51.5 us
    unnamed x1, local copies, waits for them, and re-layouts  1.67 us

profile of v1, /device:TPU:1, one launch (start us, length us, event | category | flops | bytes accessed | tf_op | source)
XLA Modules:
  0.0 53.2 jit_solution(6479931167285701541)
XLA Ops:
  0.0 51.5 %shard_map.46 = bf16[256,512]{1,0:T(8,128)(2,1)} custom-call(bf16[3,256,512]{2,1,0:T(8,128)(2,1)} %proj_hbm.1, f32[3,7,512]{2,1,0:T(8,128)} %taps_ref.1, f32[2,256]{1,0:T(2,128)} %filt_ref.1, bf16[4096,512]{1,0:T(8,128)(2,1)} %weight_hbm.1), custom_call_target="tpu_custom_call" | custom-call | tf_op jit(solution)/shard_map/pallas_call | solution.py:320
  51.5 1.7 %copy.6 = bf16[256,512]{1,0:T(8,128)(2,1)} copy(bf16[256,512]{1,0:T(8,128)(2,1)} %shard_map.46) | data formatting | bytes 524288

commit v2 on v1

v2 whole, which is shorter than its diff:
```python
import functools

import jax
import jax.numpy as jnp
from jax import lax
from jax.experimental import pallas as pl
from jax.experimental.pallas import tpu as pltpu
from jax.sharding import PartitionSpec as P

MESH = pl.DeviceIdType.MESH
TAPS = 7
PAD = 16
LANES = 128


def kernel(
    sizes,
    proj_hbm,
    taps_ref,
    filt_ref,
    weight_hbm,
    out_ref,
    proj,
    halo,
    ext,
    filt_mine,
    filt_all,
    high,
    low,
    early,
    product_out,
    product_in,
    total,
    conv_out,
    conv_in,
    query,
    gated,
    weight,
    out_total,
    load_sem,
    halo_sem,
    filt_sem,
    product_send,
    product_recv,
    conv_send,
    conv_recv,
    gated_send,
    gated_recv,
):
    count, planes, rings = sizes
    rows = proj.shape[1]
    channels = proj.shape[2]
    share = channels // count
    blocks = channels // LANES
    per_block = count // blocks
    groups = filt_ref.shape[0]
    me = lax.axis_index("seq")
    chan = lax.axis_index("chan")
    x, z = me // rings, lax.rem(me, rings)
    y, core = chan // 2, lax.rem(chan, 2)
    heights = lax.axis_size("chan") // 2
    step_up = 1 - 2 * core
    down = lax.rem(y + step_up + heights, heights) * 2 + core
    up = lax.rem(y - step_up + heights, heights) * 2 + core
    far = lax.rem(y + 2, heights) * 2 + core
    sibling = y * 2 + 1 - core
    following = lax.rem(me + 1, count)
    mine = pl.ds(me * share, share)

    def ring_peer(dx, k):
        side = 1 - 2 * lax.rem(k, 2)
        dz = rings // 2 + side * ((k + 1) // 2)
        return lax.rem(x + dx, planes) * rings + lax.rem(z + dz, rings)

    def far_first(k):
        return ring_peer(lax.rem(k // rings + 2, planes), lax.rem(k, rings))

    def near_first(k):
        return ring_peer(k // rings, lax.rem(k, rings))

    def each_peer(order, skip, step):
        def one(k, carry):
            step(order(k))
            return carry

        lax.fori_loop(0, skip, one, 0)
        lax.fori_loop(skip + 1, count, one, 0)

    last_of = {far_first: 2 * rings + rings - 1, near_first: rings - 1}

    def to_all(order, step):
        each_peer(order, last_of[order], step)

    barrier = pltpu.get_barrier_semaphore()

    def greet(to):
        pl.semaphore_signal(barrier, inc=1, device_id={"seq": to}, device_id_type=MESH)

    to_all(far_first, greet)
    for other in (down, up, sibling):
        pl.semaphore_signal(barrier, inc=1, device_id={"chan": other}, device_id_type=MESH)

    load_pair = pltpu.make_async_copy(proj_hbm.at[1:3], proj.at[1:3], load_sem.at[0])
    load_pair.start()
    load_query = pltpu.make_async_copy(proj_hbm.at[0], proj.at[0], load_sem.at[1])
    load_query.start()
    load_weight = pltpu.make_async_copy(weight_hbm, weight, load_sem.at[2])

    for g in range(groups):
        filt_mine[g] = filt_ref[g : g + 1, :]
    filt_all[0] = jnp.zeros(filt_all.shape[1:], jnp.float32)
    for h in range(2):
        product_in[h, 0:share, :] = jnp.zeros((share, LANES), jnp.bfloat16)

    def widen(s):
        for q in range(blocks):
            ext[s, q, pl.ds(PAD, rows), :] = proj[s, :, q * LANES : (q + 1) * LANES].astype(jnp.float32)

    def short(s, q, first, size):
        lanes = pl.ds(pl.multiple_of(q * LANES, LANES), LANES)
        taps = taps_ref[s, :, lanes]
        value = taps[0:1, :] * ext[s, q, pl.ds(first + PAD, size), :]
        for j in range(1, TAPS):
            value = value + taps[j : j + 1, :] * ext[s, q, pl.ds(first + PAD - j, size), :]
        return value

    def each_block(step):
        def one(q, carry):
            step(q)
            return carry

        lax.fori_loop(0, blocks, one, 0)

    def block_rows(q):
        return pl.ds(pl.multiple_of(q * LANES, LANES), LANES)

    def late_products(q):
        value = short(1, q, LANES, LANES) * short(2, q, LANES, LANES)
        product_out[1, block_rows(q), :] = value.T.astype(jnp.bfloat16)

    def early_products(q):
        early[q, 8:, :] = short(1, q, 8, LANES - 8) * short(2, q, 8, LANES - 8)

    def send_products(h):
        def send(to):
            pltpu.make_async_remote_copy(
                src_ref=product_out.at[h, pl.ds(to * share, share), :],
                dst_ref=product_in.at[h, pl.ds((me + 1) * share, share), :],
                send_sem=product_send.at[0],
                recv_sem=product_recv.at[h],
                device_id={"seq": to},
                device_id_type=MESH,
            ).start()

        to_all(far_first, send)
        pltpu.make_async_copy(
            product_out.at[h, mine, :],
            product_in.at[h, pl.ds((me + 1) * share, share), :],
            product_recv.at[h],
        ).start()

    load_pair.wait()
    widen(1)
    widen(2)
    each_block(late_products)

    pl.semaphore_wait(barrier, count + 2)

    halo_copy = pltpu.make_async_remote_copy(
        src_ref=proj_hbm.at[:, pl.ds(rows - PAD, PAD), :],
        dst_ref=halo,
        send_sem=halo_sem.at[0],
        recv_sem=halo_sem.at[1],
        device_id={"seq": following},
        device_id_type=MESH,
    )
    halo_copy.start()

    def send_filter(to):
        pltpu.make_async_remote_copy(
            src_ref=filt_mine.at[to // (count // groups)],
            dst_ref=filt_all.at[me + 1],
            send_sem=filt_sem.at[0],
            recv_sem=filt_sem.at[1],
            device_id={"seq": to},
            device_id_type=MESH,
        ).start()

    to_all(far_first, send_filter)
    pltpu.make_async_copy(
        filt_mine.at[me // (count // groups)], filt_all.at[me + 1], filt_sem.at[1]
    ).start()
    send_products(1)

    each_block(early_products)
    halo_copy.wait()
    for s in (1, 2, 0):
        for q in range(blocks):
            before = halo[s, :, q * LANES : (q + 1) * LANES].astype(jnp.float32)
            ext[s, q, 0:PAD, :] = jnp.where(me == 0, 0.0, before)

    def first_products(q):
        early[q, 0:8, :] = short(1, q, 0, 8) * short(2, q, 0, 8)
        product_out[0, block_rows(q), :] = early[q].T.astype(jnp.bfloat16)

    each_block(first_products)
    send_products(0)
    load_weight.start()

    load_query.wait()
    widen(0)

    def queries(q):
        for first in (0, LANES):
            query[q, first : first + LANES, :] = short(0, q, first, LANES)

    each_block(queries)

    def spread(d):
        line = jnp.concatenate([filt_all[d][:, rows - LANES :], filt_all[d + 1]], axis=1)
        wide = jnp.broadcast_to(line, (LANES, line.shape[1]))
        value = pltpu.roll(wide, 0, 1, stride=1, stride_axis=0)[:, LANES:]
        top = value.astype(jnp.bfloat16)
        high[d] = top
        low[d] = (value - top.astype(jnp.float32)).astype(jnp.bfloat16)

    def lagged(table, d, h):
        if h == 0:
            return table[d]
        before = table[d - 1][:, LANES:] if d else jnp.zeros((LANES, LANES), jnp.bfloat16)
        return jnp.concatenate([before, table[d][:, :LANES]], axis=1)

    def convolve(d, h):
        size = channels - share * d
        left = jnp.concatenate(
            [product_in[h, share : share + size, :], product_in[h, 0:size, :]], axis=1
        )
        part = None
        for table in (high, low):
            right = jnp.concatenate([lagged(table, d, h), lagged(table, d + 1, h)], axis=0)
            more = jnp.dot(left, right, preferred_element_type=jnp.float32)
            part = more if part is None else part + more
        if d == 0 and h == 1:
            total[...] = part
        else:
            total[share * d :, :] += part

    pltpu.make_async_copy(
        filt_all.at[pl.ds(1, count)], filt_all.at[pl.ds(1, count)], filt_sem.at[1]
    ).wait()
    whole = product_in.at[1, pl.ds(share, channels), :]
    pltpu.make_async_copy(whole, whole, product_recv.at[1]).wait()
    for d in range(0, count, 2):
        spread(d)
        spread(d + 1)
        convolve(d, 1)
    whole = product_in.at[0, pl.ds(share, channels), :]
    pltpu.make_async_copy(whole, whole, product_recv.at[0]).wait()
    for d in range(0, count, 2):
        convolve(d, 0)
    conv_out[...] = total[...].astype(jnp.bfloat16)

    def send_back(to):
        pltpu.make_async_remote_copy(
            src_ref=conv_out.at[pl.ds(to * share, share), :],
            dst_ref=conv_in.at[mine, :],
            send_sem=conv_send.at[0],
            recv_sem=conv_recv.at[me // per_block],
            device_id={"seq": to},
            device_id_type=MESH,
        ).start()

    to_all(near_first, send_back)
    pltpu.make_async_copy(conv_out.at[mine], conv_in.at[mine], conv_recv.at[me // per_block]).start()

    def pass_on(source, block, to):
        pltpu.make_async_remote_copy(
            src_ref=gated.at[source, block],
            dst_ref=gated.at[source, block],
            send_sem=gated_send.at[0],
            recv_sem=gated_recv.at[source, block],
            device_id={"chan": to},
            device_id_type=MESH,
        ).start()

    def arrived(source, block):
        slot = gated.at[source, block]
        pltpu.make_async_copy(slot, slot, gated_recv.at[source, block]).wait()

    def block_at(k):
        return lax.rem(x + blocks - k, blocks)

    def gate(k):
        block = block_at(k)
        part = block_rows(block)
        pltpu.make_async_copy(conv_in.at[part], conv_in.at[part], conv_recv.at[block]).wait()
        value = conv_in[part, :].astype(jnp.float32).T
        gated[chan, block] = (value * query[block]).astype(jnp.bfloat16)
        for to in (down, up, sibling):
            pass_on(chan, block, to)

    def relay_near(k):
        block = block_at(k)
        arrived(up, block)
        pass_on(up, block, down)
        pass_on(up, block, sibling)
        arrived(down, block)
        pass_on(down, block, sibling)

    def relay_far(k):
        block = block_at(k)
        arrived(far, block)
        pass_on(far, block, sibling)

    def project(k):
        block = block_at(k)
        for offset in range(heights):
            arrived(lax.rem(y + offset, heights) * 2 + 1 - core, block)
        left = jnp.concatenate([gated[c, block] for c in range(2 * heights)], axis=1)
        right = jnp.concatenate(
            [
                weight[pl.ds(pl.multiple_of(c * channels + block * LANES, LANES), LANES), :]
                for c in range(2 * heights)
            ],
            axis=0,
        )
        part = jnp.dot(left, right, preferred_element_type=jnp.float32)
        if k == 0:
            out_total[...] = part
        elif k < blocks - 1:
            out_total[...] += part
        else:
            out_ref[...] = (out_total[...] + part).astype(jnp.bfloat16)

    load_weight.wait()
    steps = (
        (gate, 0), (gate, 1), (gate, 2), (relay_near, 0), (gate, 3), (relay_near, 1),
        (relay_near, 2), (relay_far, 0), (relay_near, 3), (relay_far, 1), (project, 0),
        (relay_far, 2), (project, 1), (relay_far, 3), (project, 2), (project, 3),
    )
    for step, k in steps:
        step(k)

    sent = product_out.at[0:2, pl.ds(0, (count - 1) * share), :]
    pltpu.make_async_copy(sent, sent, product_send.at[0]).wait()
    sent = conv_out.at[pl.ds(0, (count - 1) * share), :]
    pltpu.make_async_copy(sent, sent, conv_send.at[0]).wait()
    sent = filt_all.at[pl.ds(1, count - 1)]
    pltpu.make_async_copy(sent, sent, filt_sem.at[0]).wait()
    sent = gated.at[pl.ds(0, 7)]
    pltpu.make_async_copy(sent, sent, gated_send.at[0]).wait()


def solution(mesh):
    count = mesh.shape["seq"]
    chans = mesh.shape["chan"]
    planes, rings = 4, count // 4

    def per_device(projections, short_taps, filters, out_weight):
        rows, channels = projections.shape[1], projections.shape[2]
        blocks = channels // LANES
        share = channels // count
        vmem = pl.BlockSpec(memory_space=pltpu.VMEM)
        hbm = pl.BlockSpec(memory_space=pl.ANY)
        bf16, f32 = jnp.bfloat16, jnp.float32
        dma = pltpu.SemaphoreType.DMA
        return pl.pallas_call(
            functools.partial(kernel, (count, planes, rings)),
            out_shape=jax.ShapeDtypeStruct((rows, out_weight.shape[1]), bf16),
            in_specs=[hbm, vmem, vmem, hbm],
            out_specs=vmem,
            scratch_shapes=[
                pltpu.VMEM(projections.shape, bf16),
                pltpu.VMEM((3, PAD, channels), bf16),
                pltpu.VMEM((3, blocks, PAD + rows, LANES), f32),
                pltpu.VMEM((filters.shape[0], 1, rows), f32),
                pltpu.VMEM((count + 1, 1, rows), f32),
                pltpu.VMEM((count, LANES, rows), bf16),
                pltpu.VMEM((count, LANES, rows), bf16),
                pltpu.VMEM((blocks, LANES, LANES), f32),
                pltpu.VMEM((2, channels, LANES), bf16),
                pltpu.VMEM((2, share + channels, LANES), bf16),
                pltpu.VMEM((channels, rows), f32),
                pltpu.VMEM((channels, rows), bf16),
                pltpu.VMEM((channels, rows), bf16),
                pltpu.VMEM((blocks, rows, LANES), f32),
                pltpu.VMEM((chans, blocks, rows, LANES), bf16),
                pltpu.VMEM(out_weight.shape, bf16),
                pltpu.VMEM((rows, out_weight.shape[1]), f32),
                dma((3,)),
                dma((2,)),
                dma((2,)),
                dma((1,)),
                dma((2,)),
                dma((1,)),
                dma((blocks,)),
                dma((1,)),
                dma((chans, blocks)),
            ],
            compiler_params=pltpu.CompilerParams(
                collective_id=0, has_side_effects=True, vmem_limit_bytes=56 * 2**20
            ),
        )(projections, short_taps, filters, out_weight)

    return jax.shard_map(
        per_device,
        mesh=mesh,
        in_specs=(P(None, "seq", "chan"), P(None, None, "chan"), P("chan", "seq"), P(None, "chan")),
        out_specs=P("seq", "chan"),
        check_vma=False,
    )
```

time: 53.4 us -> 47.7 us (0.89)
  Pallas kernels: 51.5 us -> 45.9 us
    pallas_call x1, Pallas kernels: 51.5 us -> 45.9 us  [per_device(): pl.pallas_call(functools.partial(kernel, (count, planes, rings)), out_sha...]
where the time goes in v2:
time: 47.7 us; the launch traced here: 47.5 us
  Pallas kernels  45.9 us (96%)
  local copies, waits for them, and re-layouts  1.67 us (4%)
    pallas_call x1, Pallas kernels, per_device(): pl.pallas_call(functools.partial(kernel, (count, planes, rings)), out_sha...  45.9 us
    unnamed x1, local copies, waits for them, and re-layouts  1.67 us

profile of v2, /device:TPU:1, one launch (start us, length us, event | category | flops | bytes accessed | tf_op | source)
XLA Modules:
  0.0 47.5 jit_solution(16123522290284918110)
XLA Ops:
  0.0 45.9 %shard_map.46 = bf16[256,512]{1,0:T(8,128)(2,1)} custom-call(bf16[3,256,512]{2,1,0:T(8,128)(2,1)} %proj_hbm.1, f32[3,7,512]{2,1,0:T(8,128)} %taps_ref.1, f32[2,256]{1,0:T(2,128)} %filt_ref.1, bf16[4096,512]{1,0:T(8,128)(2,1)} %weight_hbm.1), custom_call_target="tpu_custom_call" | custom-call | tf_op jit(solution)/shard_map/pallas_call | solution.py:367
  45.9 1.7 %copy.6 = bf16[256,512]{1,0:T(8,128)(2,1)} copy(bf16[256,512]{1,0:T(8,128)(2,1)} %shard_map.46) | data formatting | bytes 524288

commit v3 on v2

--- a/solution.py
+++ b/solution.py
@@ -16,10 +16,12 @@
 def kernel(
     sizes,
     proj_hbm,
+    taps_hbm,
+    filt_hbm,
+    weight_hbm,
+    out_ref,
     taps_ref,
     filt_ref,
-    weight_hbm,
-    out_ref,
     proj,
     halo,
     ext,
@@ -100,17 +102,18 @@
     for other in (down, up, sibling):
         pl.semaphore_signal(barrier, inc=1, device_id={"chan": other}, device_id_type=MESH)
 
+    load_taps = pltpu.make_async_copy(taps_hbm, taps_ref, load_sem.at[3])
+    load_taps.start()
+    load_filt = pltpu.make_async_copy(filt_hbm, filt_ref, load_sem.at[4])
+    load_filt.start()
     load_pair = pltpu.make_async_copy(proj_hbm.at[1:3], proj.at[1:3], load_sem.at[0])
     load_pair.start()
     load_query = pltpu.make_async_copy(proj_hbm.at[0], proj.at[0], load_sem.at[1])
     load_query.start()
     load_weight = pltpu.make_async_copy(weight_hbm, weight, load_sem.at[2])
 
-    for g in range(groups):
-        filt_mine[g] = filt_ref[g : g + 1, :]
-    filt_all[0] = jnp.zeros(filt_all.shape[1:], jnp.float32)
     for h in range(2):
-        product_in[h, 0:share, :] = jnp.zeros((share, LANES), jnp.bfloat16)
+        product_in[h, 0:LANES, :] = jnp.zeros((LANES, LANES), jnp.bfloat16)
 
     def widen(s):
         for q in range(blocks):
@@ -145,7 +148,7 @@
         def send(to):
             pltpu.make_async_remote_copy(
                 src_ref=product_out.at[h, pl.ds(to * share, share), :],
-                dst_ref=product_in.at[h, pl.ds((me + 1) * share, share), :],
+                dst_ref=product_in.at[h, pl.ds(LANES + me * share, share), :],
                 send_sem=product_send.at[0],
                 recv_sem=product_recv.at[h],
                 device_id={"seq": to},
@@ -155,26 +158,34 @@
         to_all(far_first, send)
         pltpu.make_async_copy(
             product_out.at[h, mine, :],
-            product_in.at[h, pl.ds((me + 1) * share, share), :],
+            product_in.at[h, pl.ds(LANES + me * share, share), :],
             product_recv.at[h],
         ).start()
 
+    load_taps.wait()
     load_pair.wait()
     widen(1)
     widen(2)
     each_block(late_products)
 
+    load_filt.wait()
+    for g in range(groups):
+        filt_mine[g] = filt_ref[g : g + 1, :]
+    filt_all[0] = jnp.zeros(filt_all.shape[1:], jnp.float32)
     pl.semaphore_wait(barrier, count + 2)
 
-    halo_copy = pltpu.make_async_remote_copy(
-        src_ref=proj_hbm.at[:, pl.ds(rows - PAD, PAD), :],
-        dst_ref=halo,
-        send_sem=halo_sem.at[0],
-        recv_sem=halo_sem.at[1],
-        device_id={"seq": following},
-        device_id_type=MESH,
-    )
-    halo_copy.start()
+    def halo_of(part, at):
+        return pltpu.make_async_remote_copy(
+            src_ref=proj.at[part, pl.ds(rows - PAD, PAD), :],
+            dst_ref=halo.at[part],
+            send_sem=halo_sem.at[at],
+            recv_sem=halo_sem.at[at + 1],
+            device_id={"seq": following},
+            device_id_type=MESH,
+        )
+
+    pair_halo = halo_of(pl.ds(1, 2), 0)
+    pair_halo.start()
 
     def send_filter(to):
         pltpu.make_async_remote_copy(
@@ -193,12 +204,15 @@
     send_products(1)
 
     each_block(early_products)
-    halo_copy.wait()
-    for s in (1, 2, 0):
+    def extend(s):
         for q in range(blocks):
             before = halo[s, :, q * LANES : (q + 1) * LANES].astype(jnp.float32)
             ext[s, q, 0:PAD, :] = jnp.where(me == 0, 0.0, before)
 
+    pair_halo.wait()
+    extend(1)
+    extend(2)
+
     def first_products(q):
         early[q, 0:8, :] = short(1, q, 0, 8) * short(2, q, 0, 8)
         product_out[0, block_rows(q), :] = early[q].T.astype(jnp.bfloat16)
@@ -207,8 +221,12 @@
     send_products(0)
     load_weight.start()
 
+    query_halo = halo_of(0, 2)
     load_query.wait()
+    query_halo.start()
     widen(0)
+    query_halo.wait()
+    extend(0)
 
     def queries(q):
         for first in (0, LANES):
@@ -224,42 +242,62 @@
         high[d] = top
         low[d] = (value - top.astype(jnp.float32)).astype(jnp.bfloat16)
 
-    def lagged(table, d, h):
-        if h == 0:
-            return table[d]
+    def lagged(table, d):
         before = table[d - 1][:, LANES:] if d else jnp.zeros((LANES, LANES), jnp.bfloat16)
         return jnp.concatenate([before, table[d][:, :LANES]], axis=1)
 
-    def convolve(d, h):
+    def convolve_late(d):
         size = channels - share * d
         left = jnp.concatenate(
-            [product_in[h, share : share + size, :], product_in[h, 0:size, :]], axis=1
+            [
+                product_in[1, LANES : LANES + size, :],
+                product_in[1, LANES - share : LANES - share + size, :],
+            ],
+            axis=1,
         )
         part = None
         for table in (high, low):
-            right = jnp.concatenate([lagged(table, d, h), lagged(table, d + 1, h)], axis=0)
+            right = jnp.concatenate([lagged(table, d), lagged(table, d + 1)], axis=0)
             more = jnp.dot(left, right, preferred_element_type=jnp.float32)
             part = more if part is None else part + more
-        if d == 0 and h == 1:
+        if d == 0:
             total[...] = part
         else:
             total[share * d :, :] += part
 
+    def convolve_early(block):
+        base = pl.multiple_of(block * LANES, LANES)
+
+        def lags(step, value):
+            for e in range(0, per_block, 2):
+                d = step * per_block + e
+                first = LANES + base - share * d
+                left = jnp.concatenate(
+                    [
+                        product_in[0, pl.ds(pl.multiple_of(first, share), LANES), :],
+                        product_in[0, pl.ds(pl.multiple_of(first - share, share), LANES), :],
+                    ],
+                    axis=1,
+                )
+                for table in (high, low):
+                    right = table[pl.ds(d, 2)].reshape(2 * LANES, rows)
+                    value = value + jnp.dot(left, right, preferred_element_type=jnp.float32)
+            return value
+
+        value = lax.fori_loop(0, block + 1, lags, total[pl.ds(base, LANES), :])
+        conv_out[pl.ds(base, LANES), :] = value.astype(jnp.bfloat16)
+
     pltpu.make_async_copy(
         filt_all.at[pl.ds(1, count)], filt_all.at[pl.ds(1, count)], filt_sem.at[1]
     ).wait()
-    whole = product_in.at[1, pl.ds(share, channels), :]
+    whole = product_in.at[1, pl.ds(LANES, channels), :]
     pltpu.make_async_copy(whole, whole, product_recv.at[1]).wait()
     for d in range(0, count, 2):
         spread(d)
         spread(d + 1)
-        convolve(d, 1)
-    whole = product_in.at[0, pl.ds(share, channels), :]
+        convolve_late(d)
+    whole = product_in.at[0, pl.ds(LANES, channels), :]
     pltpu.make_async_copy(whole, whole, product_recv.at[0]).wait()
-    for d in range(0, count, 2):
-        convolve(d, 0)
-    conv_out[...] = total[...].astype(jnp.bfloat16)
-
     def send_back(to):
         pltpu.make_async_remote_copy(
             src_ref=conv_out.at[pl.ds(to * share, share), :],
@@ -270,8 +308,17 @@
             device_id_type=MESH,
         ).start()
 
-    to_all(near_first, send_back)
-    pltpu.make_async_copy(conv_out.at[mine], conv_in.at[mine], conv_recv.at[me // per_block]).start()
+    for k in range(blocks):
+        convolve_early(lax.rem(x + k, blocks))
+
+        def one(i, carry):
+            send_back(near_first(k * rings + i))
+            return carry
+
+        lax.fori_loop(0, rings - 1 if k == 0 else rings, one, 0)
+        if k == 0:
+            own = conv_recv.at[me // per_block]
+            pltpu.make_async_copy(conv_out.at[mine], conv_in.at[mine], own).start()
 
     def pass_on(source, block, to):
         pltpu.make_async_remote_copy(
@@ -296,14 +343,20 @@
         pltpu.make_async_copy(conv_in.at[part], conv_in.at[part], conv_recv.at[block]).wait()
         value = conv_in[part, :].astype(jnp.float32).T
         gated[chan, block] = (value * query[block]).astype(jnp.bfloat16)
-        for to in (down, up, sibling):
+        for to in (down, sibling):
             pass_on(chan, block, to)
 
-    def relay_near(k):
+    def send_up(k):
+        pass_on(chan, block_at(k), up)
+
+    def near_up(k):
         block = block_at(k)
         arrived(up, block)
         pass_on(up, block, down)
         pass_on(up, block, sibling)
+
+    def near_down(k):
+        block = block_at(k)
         arrived(down, block)
         pass_on(down, block, sibling)
 
@@ -312,31 +365,47 @@
         arrived(far, block)
         pass_on(far, block, sibling)
 
-    def project(k):
-        block = block_at(k)
-        for offset in range(heights):
-            arrived(lax.rem(y + offset, heights) * 2 + 1 - core, block)
-        left = jnp.concatenate([gated[c, block] for c in range(2 * heights)], axis=1)
+    def project_part(k, stream):
+        block = block_at(k)
+        sources = [
+            lax.rem(y + offset, heights) * 2 + (1 - core if stream else core)
+            for offset in range(heights)
+        ]
+        left = jnp.concatenate([gated[c, block] for c in sources], axis=1)
         right = jnp.concatenate(
             [
                 weight[pl.ds(pl.multiple_of(c * channels + block * LANES, LANES), LANES), :]
-                for c in range(2 * heights)
+                for c in sources
             ],
             axis=0,
         )
-        part = jnp.dot(left, right, preferred_element_type=jnp.float32)
+        return jnp.dot(left, right, preferred_element_type=jnp.float32)
+
+    def project_mine(k):
+        part = project_part(k, 0)
         if k == 0:
             out_total[...] = part
-        elif k < blocks - 1:
+        else:
+            out_total[...] += part
+
+    def project_other(k):
+        block = block_at(k)
+        for offset in range(heights):
+            arrived(lax.rem(y + offset, heights) * 2 + 1 - core, block)
+        part = project_part(k, 1)
+        if k < blocks - 1:
             out_total[...] += part
         else:
             out_ref[...] = (out_total[...] + part).astype(jnp.bfloat16)
 
     load_weight.wait()
     steps = (
-        (gate, 0), (gate, 1), (gate, 2), (relay_near, 0), (gate, 3), (relay_near, 1),
-        (relay_near, 2), (relay_far, 0), (relay_near, 3), (relay_far, 1), (project, 0),
-        (relay_far, 2), (project, 1), (relay_far, 3), (project, 2), (project, 3),
+        (gate, 0), (send_up, 0), (gate, 1), (send_up, 1), (gate, 2),
+        (send_up, 2), (gate, 3), (send_up, 3), (near_up, 0), (near_up, 1),
+        (near_up, 2), (near_up, 3), (near_down, 0), (near_down, 1), (near_down, 2),
+        (near_down, 3), (relay_far, 0), (relay_far, 1), (project_mine, 0), (relay_far, 2),
+        (project_other, 0), (project_mine, 1), (relay_far, 3), (project_other, 1), (project_mine, 2),
+        (project_mine, 3), (project_other, 2), (project_other, 3),
     )
     for step, k in steps:
         step(k)
@@ -367,9 +436,11 @@
         return pl.pallas_call(
             functools.partial(kernel, (count, planes, rings)),
             out_shape=jax.ShapeDtypeStruct((rows, out_weight.shape[1]), bf16),
-            in_specs=[hbm, vmem, vmem, hbm],
+            in_specs=[hbm, hbm, hbm, hbm],
             out_specs=vmem,
             scratch_shapes=[
+                pltpu.VMEM(short_taps.shape, f32),
+                pltpu.VMEM(filters.shape, f32),
                 pltpu.VMEM(projections.shape, bf16),
                 pltpu.VMEM((3, PAD, channels), bf16),
                 pltpu.VMEM((3, blocks, PAD + rows, LANES), f32),
@@ -379,7 +450,7 @@
                 pltpu.VMEM((count, LANES, rows), bf16),
                 pltpu.VMEM((blocks, LANES, LANES), f32),
                 pltpu.VMEM((2, channels, LANES), bf16),
-                pltpu.VMEM((2, share + channels, LANES), bf16),
+                pltpu.VMEM((2, LANES + channels, LANES), bf16),
                 pltpu.VMEM((channels, rows), f32),
                 pltpu.VMEM((channels, rows), bf16),
                 pltpu.VMEM((channels, rows), bf16),
@@ -387,8 +458,8 @@
                 pltpu.VMEM((chans, blocks, rows, LANES), bf16),
                 pltpu.VMEM(out_weight.shape, bf16),
                 pltpu.VMEM((rows, out_weight.shape[1]), f32),
-                dma((3,)),
-                dma((2,)),
+                dma((5,)),
+                dma((4,)),
                 dma((2,)),
                 dma((1,)),
                 dma((2,)),
@@ -398,7 +469,7 @@
                 dma((chans, blocks)),
             ],
             compiler_params=pltpu.CompilerParams(
-                collective_id=0, has_side_effects=True, vmem_limit_bytes=56 * 2**20
+                collective_id=0, has_side_effects=True, vmem_limit_bytes=53 * 2**20
             ),
         )(projections, short_taps, filters, out_weight)
 

time: 47.7 us -> 44.9 us (0.941)
  Pallas kernels: 45.9 us -> 42.5 us
  local copies, waits for them, and re-layouts: 1.67 us -> 2.18 us
    pallas_call x1, Pallas kernels: 45.9 us -> 42.5 us  [per_device(): pl.pallas_call(functools.partial(kernel, (count, planes, rings)), out_sha...]
    unnamed x1 -> x5, local copies, waits for them, and re-layouts: 1.67 us -> 2.18 us
where the time goes in v3:
time: 44.9 us; the launch traced here: 44.7 us
  Pallas kernels  42.5 us (95%)
  local copies, waits for them, and re-layouts  2.18 us (5%)
    pallas_call x1, Pallas kernels, per_device(): pl.pallas_call(functools.partial(kernel, (count, planes, rings)), out_sha...  42.5 us
    unnamed x5, local copies, waits for them, and re-layouts  2.18 us

profile of v3, /device:TPU:1, one launch (start us, length us, event | category | flops | bytes accessed | tf_op | source)
XLA Modules:
  0.0 44.7 jit_solution(1353613888705994637)
XLA Ops:
  0.0 0.0 copy-start
  0.0 0.8 %copy-done = f32[3,7,512]{2,1,0:T(8,128)S(1)} copy-done((f32[3,7,512]{2,1,0:T(8,128)S(1)}, f32[3,7,512]{2,1,0:T(8,128)}, u32[]{:S(2)}) %copy-start) | copy-done | bytes 43032
  0.8 0.0 copy-start.1
  0.8 0.7 %copy-done.1 = f32[2,256]{1,0:T(2,128)S(1)} copy-done((f32[2,256]{1,0:T(2,128)S(1)}, f32[2,256]{1,0:T(2,128)}, u32[]{:S(2)}) %copy-start.1) | copy-done | bytes 2072
  1.5 42.5 %shard_map.46 = bf16[256,512]{1,0:T(8,128)(2,1)S(1)} custom-call(bf16[3,256,512]{2,1,0:T(8,128)(2,1)} %proj_hbm.1, f32[3,7,512]{2,1,0:T(8,128)S(1)} %copy-done, f32[2,256]{1,0:T(2,128)S(1)} %copy-done.1, bf16[4096,512]{1,0:T(8,128)(2,1)} %weight_hbm.1), custom_call_target="tpu_custom_call" | custom-call | tf_op jit(solution)/shard_map/pallas_call | solution.py:436
  44.0 0.7 %copy.6 = bf16[256,512]{1,0:T(8,128)(2,1)} copy(bf16[256,512]{1,0:T(8,128)(2,1)S(1)} %shard_map.46) | data formatting | bytes 524288
Async XLA Ops:
  0.0 0.8 %copy-start = (f32[3,7,512]{2,1,0:T(8,128)S(1)}, f32[3,7,512]{2,1,0:T(8,128)}, u32[]{:S(2)}) copy-start(f32[3,7,512]{2,1,0:T(8,128)} %taps_hbm.1) | copy-start | bytes 129028
  0.8 0.7 %copy-start.1 = (f32[2,256]{1,0:T(2,128)S(1)}, f32[2,256]{1,0:T(2,128)}, u32[]{:S(2)}) copy-start(f32[2,256]{1,0:T(2,128)} %filt_hbm.1) | copy-start | bytes 6148

commit v4 on v3

--- a/solution.py
+++ b/solution.py
@@ -225,15 +225,6 @@
     load_query.wait()
     query_halo.start()
     widen(0)
-    query_halo.wait()
-    extend(0)
-
-    def queries(q):
-        for first in (0, LANES):
-            query[q, first : first + LANES, :] = short(0, q, first, LANES)
-
-    each_block(queries)
-
     def spread(d):
         line = jnp.concatenate([filt_all[d][:, rows - LANES :], filt_all[d + 1]], axis=1)
         wide = jnp.broadcast_to(line, (LANES, line.shape[1]))
@@ -279,7 +270,7 @@
                     ],
                     axis=1,
                 )
-                for table in (high, low):
+                for table in (high,):
                     right = table[pl.ds(d, 2)].reshape(2 * LANES, rows)
                     value = value + jnp.dot(left, right, preferred_element_type=jnp.float32)
             return value
@@ -290,12 +281,21 @@
     pltpu.make_async_copy(
         filt_all.at[pl.ds(1, count)], filt_all.at[pl.ds(1, count)], filt_sem.at[1]
     ).wait()
+    for d in range(count):
+        spread(d)
     whole = product_in.at[1, pl.ds(LANES, channels), :]
     pltpu.make_async_copy(whole, whole, product_recv.at[1]).wait()
     for d in range(0, count, 2):
-        spread(d)
-        spread(d + 1)
         convolve_late(d)
+    query_halo.wait()
+    extend(0)
+
+    def queries(q):
+        for first in (0, LANES):
+            query[q, first : first + LANES, :] = short(0, q, first, LANES)
+
+    each_block(queries)
+
     whole = product_in.at[0, pl.ds(LANES, channels), :]
     pltpu.make_async_copy(whole, whole, product_recv.at[0]).wait()
     def send_back(to):
@@ -399,14 +399,7 @@
             out_ref[...] = (out_total[...] + part).astype(jnp.bfloat16)
 
     load_weight.wait()
-    steps = (
-        (gate, 0), (send_up, 0), (gate, 1), (send_up, 1), (gate, 2),
-        (send_up, 2), (gate, 3), (send_up, 3), (near_up, 0), (near_up, 1),
-        (near_up, 2), (near_up, 3), (near_down, 0), (near_down, 1), (near_down, 2),
-        (near_down, 3), (relay_far, 0), (relay_far, 1), (project_mine, 0), (relay_far, 2),
-        (project_other, 0), (project_mine, 1), (relay_far, 3), (project_other, 1), (project_mine, 2),
-        (project_mine, 3), (project_other, 2), (project_other, 3),
-    )
+    steps = ((gate, 0), (send_up, 0), (gate, 1), (send_up, 1), (gate, 2), (send_up, 2), (gate, 3), (send_up, 3), (near_up, 0), (near_up, 1), (near_up, 2), (near_up, 3), (near_down, 0), (near_down, 1), (near_down, 2), (near_down, 3), (relay_far, 0), (relay_far, 1), (project_mine, 0), (project_other, 0), (relay_far, 2), (project_mine, 1), (project_other, 1), (project_mine, 2), (relay_far, 3), (project_other, 2), (project_mine, 3), (project_other, 3))
     for step, k in steps:
         step(k)
 
@@ -469,9 +462,9 @@
                 dma((chans, blocks)),
             ],
             compiler_params=pltpu.CompilerParams(
-                collective_id=0, has_side_effects=True, vmem_limit_bytes=53 * 2**20
+                collective_id=0, has_side_effects=True, vmem_limit_bytes=24 * 2**20
             ),
-        )(projections, short_taps, filters, out_weight)
+        )(*[pltpu.with_memory_space_constraint(a, pltpu.HBM) for a in (projections, short_taps, filters, out_weight)])
 
     return jax.shard_map(
         per_device,

time: 44.9 us -> 42 us (0.935)
  local copies, waits for them, and re-layouts: 2.18 us -> 0.71 us
  Pallas kernels: 42.5 us -> 41.2 us
    unnamed x5 -> x1, local copies, waits for them, and re-layouts: 2.18 us -> 0.71 us
    pallas_call x1, Pallas kernels: 42.5 us -> 41.2 us  [per_device(): pl.pallas_call(functools.partial(kernel, (count, planes, rings)), out_sha...]
where the time goes in v4:
time: 42 us; the launch traced here: 41.9 us
  Pallas kernels  41.2 us (98%)
  local copies, waits for them, and re-layouts  0.71 us (2%)
    pallas_call x1, Pallas kernels, per_device(): pl.pallas_call(functools.partial(kernel, (count, planes, rings)), out_sha...  41.2 us

profile of v4, /device:TPU:1, one launch (start us, length us, event | category | flops | bytes accessed | tf_op | source)
XLA Modules:
  0.0 41.9 jit_solution(15652652823385466419)
XLA Ops:
  0.0 41.2 %shard_map.46 = bf16[256,512]{1,0:T(8,128)(2,1)S(1)} custom-call(bf16[3,256,512]{2,1,0:T(8,128)(2,1)} %proj_hbm.1, f32[3,7,512]{2,1,0:T(8,128)} %taps_hbm.1, f32[2,256]{1,0:T(2,128)} %filt_hbm.1, bf16[4096,512]{1,0:T(8,128)(2,1)} %weight_hbm.1), custom_call_target="tpu_custom_call" | custom-call | tf_op jit(solution)/shard_map/pallas_call | solution.py:429
  41.2 0.7 %copy.6 = bf16[256,512]{1,0:T(8,128)(2,1)} copy(bf16[256,512]{1,0:T(8,128)(2,1)S(1)} %shard_map.46) | data formatting | bytes 524288

commit v5 on v4

--- a/solution.py
+++ b/solution.py
@@ -9,6 +9,7 @@
 
 MESH = pl.DeviceIdType.MESH
 TAPS = 7
+BACK_ORDER = (0, 2, 1, 3)
 PAD = 16
 LANES = 128
 
@@ -24,6 +25,8 @@
     filt_ref,
     proj,
     halo,
+    edge_out,
+    edge_in,
     ext,
     filt_mine,
     filt_all,
@@ -144,18 +147,17 @@
     def early_products(q):
         early[q, 8:, :] = short(1, q, 8, LANES - 8) * short(2, q, 8, LANES - 8)
 
-    def send_products(h):
-        def send(to):
-            pltpu.make_async_remote_copy(
-                src_ref=product_out.at[h, pl.ds(to * share, share), :],
-                dst_ref=product_in.at[h, pl.ds(LANES + me * share, share), :],
-                send_sem=product_send.at[0],
-                recv_sem=product_recv.at[h],
-                device_id={"seq": to},
-                device_id_type=MESH,
-            ).start()
-
-        to_all(far_first, send)
+    def send_product(h, to):
+        pltpu.make_async_remote_copy(
+            src_ref=product_out.at[h, pl.ds(to * share, share), :],
+            dst_ref=product_in.at[h, pl.ds(LANES + me * share, share), :],
+            send_sem=product_send.at[0],
+            recv_sem=product_recv.at[h],
+            device_id={"seq": to},
+            device_id_type=MESH,
+        ).start()
+
+    def keep_product(h):
         pltpu.make_async_copy(
             product_out.at[h, mine, :],
             product_in.at[h, pl.ds(LANES + me * share, share), :],
@@ -172,19 +174,23 @@
     for g in range(groups):
         filt_mine[g] = filt_ref[g : g + 1, :]
     filt_all[0] = jnp.zeros(filt_all.shape[1:], jnp.float32)
+    for q in range(blocks):
+        edge = [ext[s, q, pl.ds(PAD + rows - 8, 8), :] for s in (1, 2)]
+        edge_out[:, q * LANES : (q + 1) * LANES] = jnp.concatenate(edge, axis=0).astype(jnp.bfloat16)
+
     pl.semaphore_wait(barrier, count + 2)
 
-    def halo_of(part, at):
+    def halo_of(source, target, at):
         return pltpu.make_async_remote_copy(
-            src_ref=proj.at[part, pl.ds(rows - PAD, PAD), :],
-            dst_ref=halo.at[part],
+            src_ref=source,
+            dst_ref=target,
             send_sem=halo_sem.at[at],
             recv_sem=halo_sem.at[at + 1],
             device_id={"seq": following},
             device_id_type=MESH,
         )
 
-    pair_halo = halo_of(pl.ds(1, 2), 0)
+    pair_halo = halo_of(edge_out, edge_in, 0)
     pair_halo.start()
 
     def send_filter(to):
@@ -201,27 +207,35 @@
     pltpu.make_async_copy(
         filt_mine.at[me // (count // groups)], filt_all.at[me + 1], filt_sem.at[1]
     ).start()
-    send_products(1)
+    to_all(far_first, functools.partial(send_product, 1))
+    keep_product(1)
 
     each_block(early_products)
-    def extend(s):
-        for q in range(blocks):
-            before = halo[s, :, q * LANES : (q + 1) * LANES].astype(jnp.float32)
-            ext[s, q, 0:PAD, :] = jnp.where(me == 0, 0.0, before)
-
     pair_halo.wait()
-    extend(1)
-    extend(2)
+    for q in range(blocks):
+        edge = edge_in[:, q * LANES : (q + 1) * LANES].astype(jnp.float32)
+        edge = jnp.where(me == 0, 0.0, edge)
+        ext[1, q, 8:PAD, :] = edge[0:8]
+        ext[2, q, 8:PAD, :] = edge[8:]
 
     def first_products(q):
         early[q, 0:8, :] = short(1, q, 0, 8) * short(2, q, 0, 8)
         product_out[0, block_rows(q), :] = early[q].T.astype(jnp.bfloat16)
 
-    each_block(first_products)
-    send_products(0)
+    for k in range(planes):
+        dx = (k + 2) % planes
+        first_products(lax.rem(x + dx, planes))
+
+        def one(i, carry):
+            send_product(0, ring_peer(dx, i))
+            return carry
+
+        lax.fori_loop(0, rings - 1 if dx == 0 else rings, one, 0)
+        if dx == 0:
+            keep_product(0)
     load_weight.start()
 
-    query_halo = halo_of(0, 2)
+    query_halo = halo_of(proj.at[0, pl.ds(rows - PAD, PAD), :], halo, 2)
     load_query.wait()
     query_halo.start()
     widen(0)
@@ -288,7 +302,9 @@
     for d in range(0, count, 2):
         convolve_late(d)
     query_halo.wait()
-    extend(0)
+    for q in range(blocks):
+        before = halo[:, q * LANES : (q + 1) * LANES].astype(jnp.float32)
+        ext[0, q, 0:PAD, :] = jnp.where(me == 0, 0.0, before)
 
     def queries(q):
         for first in (0, LANES):
@@ -308,15 +324,15 @@
             device_id_type=MESH,
         ).start()
 
-    for k in range(blocks):
-        convolve_early(lax.rem(x + k, blocks))
+    for dx in BACK_ORDER:
+        convolve_early(lax.rem(x + dx, blocks))
 
         def one(i, carry):
-            send_back(near_first(k * rings + i))
+            send_back(ring_peer(dx, i))
             return carry
 
-        lax.fori_loop(0, rings - 1 if k == 0 else rings, one, 0)
-        if k == 0:
+        lax.fori_loop(0, rings - 1 if dx == 0 else rings, one, 0)
+        if dx == 0:
             own = conv_recv.at[me // per_block]
             pltpu.make_async_copy(conv_out.at[mine], conv_in.at[mine], own).start()
 
@@ -335,7 +351,7 @@
         pltpu.make_async_copy(slot, slot, gated_recv.at[source, block]).wait()
 
     def block_at(k):
-        return lax.rem(x + blocks - k, blocks)
+        return lax.rem(x + blocks - BACK_ORDER[k], blocks)
 
     def gate(k):
         block = block_at(k)
@@ -365,12 +381,8 @@
         arrived(far, block)
         pass_on(far, block, sibling)
 
-    def project_part(k, stream):
+    def project_part(k, sources):
         block = block_at(k)
-        sources = [
-            lax.rem(y + offset, heights) * 2 + (1 - core if stream else core)
-            for offset in range(heights)
-        ]
         left = jnp.concatenate([gated[c, block] for c in sources], axis=1)
         right = jnp.concatenate(
             [
@@ -381,25 +393,40 @@
         )
         return jnp.dot(left, right, preferred_element_type=jnp.float32)
 
+    own_stream = (chan, up, down, far)
+    other_stream = [c + 1 - 2 * core for c in own_stream]
+
     def project_mine(k):
-        part = project_part(k, 0)
+        part = project_part(k, own_stream)
         if k == 0:
             out_total[...] = part
         else:
             out_total[...] += part
 
     def project_other(k):
-        block = block_at(k)
-        for offset in range(heights):
-            arrived(lax.rem(y + offset, heights) * 2 + 1 - core, block)
-        part = project_part(k, 1)
-        if k < blocks - 1:
-            out_total[...] += part
-        else:
-            out_ref[...] = (out_total[...] + part).astype(jnp.bfloat16)
+        for c in other_stream:
+            arrived(c, block_at(k))
+        out_total[...] += project_part(k, other_stream)
+
+    def project_near(k):
+        for c in other_stream[:3]:
+            arrived(c, block_at(k))
+        out_total[...] += project_part(k, own_stream[:3] + tuple(other_stream[:3]))
+
+    def project_rest(k):
+        arrived(other_stream[3], block_at(k))
+        part = project_part(k, (far, other_stream[3]))
+        out_ref[...] = (out_total[...] + part).astype(jnp.bfloat16)
 
     load_weight.wait()
-    steps = ((gate, 0), (send_up, 0), (gate, 1), (send_up, 1), (gate, 2), (send_up, 2), (gate, 3), (send_up, 3), (near_up, 0), (near_up, 1), (near_up, 2), (near_up, 3), (near_down, 0), (near_down, 1), (near_down, 2), (near_down, 3), (relay_far, 0), (relay_far, 1), (project_mine, 0), (project_other, 0), (relay_far, 2), (project_mine, 1), (project_other, 1), (project_mine, 2), (relay_far, 3), (project_other, 2), (project_mine, 3), (project_other, 3))
+    steps = (
+        (gate, 0), (send_up, 0), (gate, 1), (send_up, 1), (gate, 2),
+        (send_up, 2), (gate, 3), (send_up, 3), (near_up, 0), (near_up, 1),
+        (near_up, 2), (near_up, 3), (near_down, 0), (near_down, 1), (near_down, 2),
+        (near_down, 3), (relay_far, 0), (relay_far, 1), (project_mine, 0), (project_other, 0),
+        (relay_far, 2), (project_mine, 1), (project_other, 1), (project_mine, 2), (relay_far, 3),
+        (project_other, 2), (project_near, 3), (project_rest, 3),
+    )
     for step, k in steps:
         step(k)
 
@@ -435,7 +462,9 @@
                 pltpu.VMEM(short_taps.shape, f32),
                 pltpu.VMEM(filters.shape, f32),
                 pltpu.VMEM(projections.shape, bf16),
-                pltpu.VMEM((3, PAD, channels), bf16),
+                pltpu.VMEM((PAD, channels), bf16),
+                pltpu.VMEM((PAD, channels), bf16),
+                pltpu.VMEM((PAD, channels), bf16),
                 pltpu.VMEM((3, blocks, PAD + rows, LANES), f32),
                 pltpu.VMEM((filters.shape[0], 1, rows), f32),
                 pltpu.VMEM((count + 1, 1, rows), f32),

time: 42 us -> 41.5 us (0.988)
  Pallas kernels: 41.2 us -> 40.7 us
    pallas_call x1, Pallas kernels: 41.2 us -> 40.7 us  [per_device(): pl.pallas_call(functools.partial(kernel, (count, planes, rings)), out_sha...]
where the time goes in v5:
time: 41.5 us; the launch traced here: 41.4 us
  Pallas kernels  40.7 us (98%)
  local copies, waits for them, and re-layouts  0.71 us (2%)
    pallas_call x1, Pallas kernels, per_device(): pl.pallas_call(functools.partial(kernel, (count, planes, rings)), out_sha...  40.7 us

profile of v5, /device:TPU:1, one launch (start us, length us, event | category | flops | bytes accessed | tf_op | source)
XLA Modules:
  0.0 41.4 jit_solution(9939157250746421782)
XLA Ops:
  0.0 40.7 %shard_map.46 = bf16[256,512]{1,0:T(8,128)(2,1)S(1)} custom-call(bf16[3,256,512]{2,1,0:T(8,128)(2,1)} %proj_hbm.1, f32[3,7,512]{2,1,0:T(8,128)} %taps_hbm.1, f32[2,256]{1,0:T(2,128)} %filt_hbm.1, bf16[4096,512]{1,0:T(8,128)(2,1)} %weight_hbm.1), custom_call_target="tpu_custom_call" | custom-call | tf_op jit(solution)/shard_map/pallas_call | solution.py:456
  40.7 0.7 %copy.6 = bf16[256,512]{1,0:T(8,128)(2,1)} copy(bf16[256,512]{1,0:T(8,128)(2,1)S(1)} %shard_map.46) | data formatting | bytes 524288

commit v6 on v5

--- a/solution.py
+++ b/solution.py
@@ -9,6 +9,7 @@
 
 MESH = pl.DeviceIdType.MESH
 TAPS = 7
+EARLY_ORDER = (2, 3, 1, 0)
 BACK_ORDER = (0, 2, 1, 3)
 PAD = 16
 LANES = 128
@@ -152,7 +153,7 @@
             src_ref=product_out.at[h, pl.ds(to * share, share), :],
             dst_ref=product_in.at[h, pl.ds(LANES + me * share, share), :],
             send_sem=product_send.at[0],
-            recv_sem=product_recv.at[h],
+            recv_sem=product_recv.at[blocks if h else x],
             device_id={"seq": to},
             device_id_type=MESH,
         ).start()
@@ -161,7 +162,7 @@
         pltpu.make_async_copy(
             product_out.at[h, mine, :],
             product_in.at[h, pl.ds(LANES + me * share, share), :],
-            product_recv.at[h],
+            product_recv.at[blocks if h else x],
         ).start()
 
     load_taps.wait()
@@ -222,8 +223,7 @@
         early[q, 0:8, :] = short(1, q, 0, 8) * short(2, q, 0, 8)
         product_out[0, block_rows(q), :] = early[q].T.astype(jnp.bfloat16)
 
-    for k in range(planes):
-        dx = (k + 2) % planes
+    for dx in EARLY_ORDER:
         first_products(lax.rem(x + dx, planes))
 
         def one(i, carry):
@@ -270,7 +270,12 @@
         else:
             total[share * d :, :] += part
 
-    def convolve_early(block):
+    def early_arrived(dx):
+        source = lax.rem(x + blocks - dx, blocks)
+        place = product_in.at[0, pl.ds(pl.multiple_of((source + 1) * LANES, LANES), LANES), :]
+        pltpu.make_async_copy(place, place, product_recv.at[source]).wait()
+
+    def convolve_early(block, parts=None):
         base = pl.multiple_of(block * LANES, LANES)
 
         def lags(step, value):
@@ -289,7 +294,16 @@
                     value = value + jnp.dot(left, right, preferred_element_type=jnp.float32)
             return value
 
-        value = lax.fori_loop(0, block + 1, lags, total[pl.ds(base, LANES), :])
+        value = total[pl.ds(base, LANES), :]
+        if parts is None:
+            value = lax.fori_loop(0, block + 1, lags, value)
+        else:
+            for sources, steps in parts:
+                for dx in sources:
+                    early_arrived(dx)
+                for step in steps:
+                    stop = step + (block + blocks - step) // blocks
+                    value = lax.fori_loop(step, stop, lags, value)
         conv_out[pl.ds(base, LANES), :] = value.astype(jnp.bfloat16)
 
     pltpu.make_async_copy(
@@ -298,7 +312,7 @@
     for d in range(count):
         spread(d)
     whole = product_in.at[1, pl.ds(LANES, channels), :]
-    pltpu.make_async_copy(whole, whole, product_recv.at[1]).wait()
+    pltpu.make_async_copy(whole, whole, product_recv.at[blocks]).wait()
     for d in range(0, count, 2):
         convolve_late(d)
     query_halo.wait()
@@ -312,8 +326,6 @@
 
     each_block(queries)
 
-    whole = product_in.at[0, pl.ds(LANES, channels), :]
-    pltpu.make_async_copy(whole, whole, product_recv.at[0]).wait()
     def send_back(to):
         pltpu.make_async_remote_copy(
             src_ref=conv_out.at[pl.ds(to * share, share), :],
@@ -325,7 +337,10 @@
         ).start()
 
     for dx in BACK_ORDER:
-        convolve_early(lax.rem(x + dx, blocks))
+        if dx == 0:
+            convolve_early(x, (((2, 3), (2, 3)), ((1,), (1,)), ((0,), (0,))))
+        else:
+            convolve_early(lax.rem(x + dx, blocks))
 
         def one(i, carry):
             send_back(ring_peer(dx, i))
@@ -484,7 +499,7 @@
                 dma((4,)),
                 dma((2,)),
                 dma((1,)),
-                dma((2,)),
+                dma((blocks + 1,)),
                 dma((1,)),
                 dma((blocks,)),
                 dma((1,)),

time: 41.5 us -> 41.1 us (level)
  no operation moved by 1% of the time
where the time goes in v6:
time: 41.1 us
  Pallas kernels  40.3 us (98%)
  local copies, waits for them, and re-layouts  0.71 us (2%)
    pallas_call x1, Pallas kernels, per_device(): pl.pallas_call(functools.partial(kernel, (count, planes, rings)), out_sha...  40.3 us

profile of v6, /device:TPU:1, one launch (start us, length us, event | category | flops | bytes accessed | tf_op | source)
XLA Modules:
  0.0 41.1 jit_solution(7171040119952273725)
XLA Ops:
  0.0 40.3 %shard_map.46 = bf16[256,512]{1,0:T(8,128)(2,1)S(1)} custom-call(bf16[3,256,512]{2,1,0:T(8,128)(2,1)} %proj_hbm.1, f32[3,7,512]{2,1,0:T(8,128)} %taps_hbm.1, f32[2,256]{1,0:T(2,128)} %filt_hbm.1, bf16[4096,512]{1,0:T(8,128)(2,1)} %weight_hbm.1), custom_call_target="tpu_custom_call" | custom-call | tf_op jit(solution)/shard_map/pallas_call | solution.py:471
  40.3 0.7 %copy.6 = bf16[256,512]{1,0:T(8,128)(2,1)} copy(bf16[256,512]{1,0:T(8,128)(2,1)S(1)} %shard_map.46) | data formatting | bytes 524288

commit v7 on v6

--- a/solution.py
+++ b/solution.py
@@ -103,7 +103,7 @@
         pl.semaphore_signal(barrier, inc=1, device_id={"seq": to}, device_id_type=MESH)
 
     to_all(far_first, greet)
-    for other in (down, up, sibling):
+    for other in (down, up, far, sibling):
         pl.semaphore_signal(barrier, inc=1, device_id={"chan": other}, device_id_type=MESH)
 
     load_taps = pltpu.make_async_copy(taps_hbm, taps_ref, load_sem.at[3])
@@ -179,7 +179,7 @@
         edge = [ext[s, q, pl.ds(PAD + rows - 8, 8), :] for s in (1, 2)]
         edge_out[:, q * LANES : (q + 1) * LANES] = jnp.concatenate(edge, axis=0).astype(jnp.bfloat16)
 
-    pl.semaphore_wait(barrier, count + 2)
+    pl.semaphore_wait(barrier, count + 3)
 
     def halo_of(source, target, at):
         return pltpu.make_async_remote_copy(
@@ -374,7 +374,7 @@
         pltpu.make_async_copy(conv_in.at[part], conv_in.at[part], conv_recv.at[block]).wait()
         value = conv_in[part, :].astype(jnp.float32).T
         gated[chan, block] = (value * query[block]).astype(jnp.bfloat16)
-        for to in (down, sibling):
+        for to in (far, down, sibling) if k == 0 else (down, sibling):
             pass_on(chan, block, to)
 
     def send_up(k):
@@ -383,7 +383,8 @@
     def near_up(k):
         block = block_at(k)
         arrived(up, block)
-        pass_on(up, block, down)
+        if k > 0:
+            pass_on(up, block, down)
         pass_on(up, block, sibling)
 
     def near_down(k):

time: 41.1 us -> 41.1 us (level)
  no operation moved by 1% of the time
where the time goes in v7:
time: 41.1 us
  Pallas kernels  40.3 us (98%)
  local copies, waits for them, and re-layouts  0.71 us (2%)
    pallas_call x1, Pallas kernels, per_device(): pl.pallas_call(functools.partial(kernel, (count, planes, rings)), out_sha...  40.3 us

profile of v7, /device:TPU:1, one launch (start us, length us, event | category | flops | bytes accessed | tf_op | source)
XLA Modules:
  0.0 41.1 jit_solution(4061435780770021232)
XLA Ops:
  0.0 40.3 %shard_map.46 = bf16[256,512]{1,0:T(8,128)(2,1)S(1)} custom-call(bf16[3,256,512]{2,1,0:T(8,128)(2,1)} %proj_hbm.1, f32[3,7,512]{2,1,0:T(8,128)} %taps_hbm.1, f32[2,256]{1,0:T(2,128)} %filt_hbm.1, bf16[4096,512]{1,0:T(8,128)(2,1)} %weight_hbm.1), custom_call_target="tpu_custom_call" | custom-call | tf_op jit(solution)/shard_map/pallas_call | solution.py:472
  40.3 0.7 %copy.6 = bf16[256,512]{1,0:T(8,128)(2,1)} copy(bf16[256,512]{1,0:T(8,128)(2,1)S(1)} %shard_map.46) | data formatting | bytes 524288

commit v8 on v7

--- a/solution.py
+++ b/solution.py
@@ -315,17 +315,6 @@
     pltpu.make_async_copy(whole, whole, product_recv.at[blocks]).wait()
     for d in range(0, count, 2):
         convolve_late(d)
-    query_halo.wait()
-    for q in range(blocks):
-        before = halo[:, q * LANES : (q + 1) * LANES].astype(jnp.float32)
-        ext[0, q, 0:PAD, :] = jnp.where(me == 0, 0.0, before)
-
-    def queries(q):
-        for first in (0, LANES):
-            query[q, first : first + LANES, :] = short(0, q, first, LANES)
-
-    each_block(queries)
-
     def send_back(to):
         pltpu.make_async_remote_copy(
             src_ref=conv_out.at[pl.ds(to * share, share), :],
@@ -433,6 +422,17 @@
         arrived(other_stream[3], block_at(k))
         part = project_part(k, (far, other_stream[3]))
         out_ref[...] = (out_total[...] + part).astype(jnp.bfloat16)
+
+    query_halo.wait()
+    for q in range(blocks):
+        before = halo[:, q * LANES : (q + 1) * LANES].astype(jnp.float32)
+        ext[0, q, 0:PAD, :] = jnp.where(me == 0, 0.0, before)
+
+    def queries(q):
+        for first in (0, LANES):
+            query[q, first : first + LANES, :] = short(0, q, first, LANES)
+
+    each_block(queries)
 
     load_weight.wait()
     steps = (

time: 41.1 us -> 41.1 us (level)
  no operation moved by 1% of the time
where the time goes in v8:
time: 41.1 us
  Pallas kernels  40.3 us (98%)
  local copies, waits for them, and re-layouts  0.71 us (2%)
    pallas_call x1, Pallas kernels, per_device(): pl.pallas_call(functools.partial(kernel, (count, planes, rings)), out_sha...  40.3 us

profile of v8, /device:TPU:1, one launch (start us, length us, event | category | flops | bytes accessed | tf_op | source)
XLA Modules:
  0.0 41.1 jit_solution(3447986422538301741)
XLA Ops:
  0.0 40.3 %shard_map.46 = bf16[256,512]{1,0:T(8,128)(2,1)S(1)} custom-call(bf16[3,256,512]{2,1,0:T(8,128)(2,1)} %proj_hbm.1, f32[3,7,512]{2,1,0:T(8,128)} %taps_hbm.1, f32[2,256]{1,0:T(2,128)} %filt_hbm.1, bf16[4096,512]{1,0:T(8,128)(2,1)} %weight_hbm.1), custom_call_target="tpu_custom_call" | custom-call | tf_op jit(solution)/shard_map/pallas_call | solution.py:472
  40.3 0.7 %copy.6 = bf16[256,512]{1,0:T(8,128)(2,1)} copy(bf16[256,512]{1,0:T(8,128)(2,1)S(1)} %shard_map.46) | data formatting | bytes 524288
